TPU v7x, 32 devices: a whole 2x2x4 slice. The times are simulated.
32 devices in a mesh: batch: 8 (over z, y), seq: 4 (over x, core).
Axes of the slice: x: 2, y: 2, z: 4, core: 2. Of those that a mesh axis runs over, the one named last changes fastest.
Arguments:
- tokens: bfloat16 [24, 512, 768], P('batch', 'seq'), may hold values from -6 to 6
- cotangent: bfloat16 [24, 512, 768], P('batch', 'seq'), may hold values from -6 to 6
- path_masks: int32 [24, 5], P('batch'), may hold values from 0 to 1, as said below
- seg_starts: int32 [24, 4], P('batch'), may hold values from 0 to 511, as said below
- query_weight: bfloat16 [768, 768], replicated, may hold values from -0.21875 to 0.21875
- key_weight: bfloat16 [768, 768], replicated, may hold values from -0.21875 to 0.21875
- value_weight: bfloat16 [768, 768], replicated, may hold values from -0.21875 to 0.21875
- output_weight: bfloat16 [768, 768], replicated, may hold values from -1.75 to 1.75
- small_kernel: bfloat16 [3, 768], replicated, may hold values from -3.5 to 3.5
- middle_kernel: bfloat16 [5, 768], replicated, may hold values from -2.5 to 2.5
- large_kernel: bfloat16 [7, 768], replicated, may hold values from -2 to 2
- small_mixer: bfloat16 [768, 768], replicated, may hold values from -0.21875 to 0.21875
- middle_mixer: bfloat16 [768, 768], replicated, may hold values from -0.21875 to 0.21875
- large_mixer: bfloat16 [768, 768], replicated, may hold values from -0.21875 to 0.21875
- inner_weight: bfloat16 [768, 3072], replicated, may hold values from -0.21875 to 0.21875
- outer_weight: bfloat16 [3072, 768], replicated, may hold values from -0.109375 to 0.109375
- norm_gain: bfloat16 [768], replicated, may hold values from 0.5 to 1.5
- norm_bias: bfloat16 [768], replicated, may hold values from -1.5 to 1.5
Outputs:
- block_output: bfloat16 [24, 512, 768], P('batch', 'seq')
- input_grad: bfloat16 [24, 512, 768], P('batch', 'seq')
- query_grad: float32 [768, 768], P('batch')
- key_grad: float32 [768, 768], P('batch')
- value_grad: float32 [768, 768], P('batch')
- output_grad: float32 [768, 768], P('batch')
- small_kernel_grad: float32 [3, 768], P(None, 'batch')
- middle_kernel_grad: float32 [5, 768], P(None, 'batch')
- large_kernel_grad: float32 [7, 768], P(None, 'batch')
- small_mixer_grad: float32 [768, 768], P('batch')
- middle_mixer_grad: float32 [768, 768], P('batch')
- large_mixer_grad: float32 [768, 768], P('batch')
- inner_grad: float32 [768, 3072], P('batch')
- outer_grad: float32 [3072, 768], P('batch')
- gain_grad: float32 [768], P('batch')
- bias_grad: float32 [768], P('batch')
Inputs may be any that keep to these rules, and one draw needn't show every extreme that they name: `path_masks`: every entry is 0 or 1, and every column has a 1 in some row. `seg_starts`: each row begins with 0 and never falls; equal starts mean empty documents.
All inputs are finite; a program needn't handle non-finite values.
Results may differ from a plain program's by a relative error of at most 0.012.
The roundings to bfloat16 on the way count: a program that leaves them out, or rounds other values in their place, can miss the bound.
Values may be sent and summed in bfloat16 or wider, within the bound.
No kernel may reach another device: no remote copies, remote signals or barrier semaphores. Data moves between devices by JAX's collectives and lax.ppermute only.
A program may use at most 192 MiB of HBM per device.

v0:
```python
import jax
import jax.numpy as jnp
from jax import lax
from jax.sharding import PartitionSpec as P

HD = 64


EPSILON = 1e-05
MASKED = -1e30


def extended(value, sides, width):
    for axis, dim in sides:
        size, length = (lax.axis_size(axis), value.shape[dim])
        up = [(i, (i + 1) % size) for i in range(size - 1)]
        down = [(j, i) for i, j in up]
        last = lax.slice_in_dim(value, length - width, length, axis=dim)
        leading = lax.slice_in_dim(value, 0, width, axis=dim)
        before = lax.ppermute(last, axis, up)
        after = lax.ppermute(leading, axis, down)
        value = jnp.concatenate([before, value, after], axis=dim)
    return value


def document_ids(starts, positions, seq_len):
    inside = (starts[:, None, :] <= positions[None, :, None]).astype(jnp.int32)
    found = jnp.sum(inside, axis=2) - 1
    valid = (positions >= 0) & (positions < seq_len)
    return jnp.where(valid[None, :], found, -1)


def matmul(left, right):
    return jnp.dot(left, right, preferred_element_type=jnp.float32)


def matmul_tn(left, right):
    return lax.dot_general(
        left, right, (((0,), (0,)), ((), ())), preferred_element_type=jnp.float32
    )


def matmul_nt(left, right):
    return lax.dot_general(
        left, right, (((1,), (1,)), ((), ())), preferred_element_type=jnp.float32
    )


def gelu_exact(values):
    return jax.nn.gelu(values, approximate=False)


def head_scores(query_seq, keys_seq, query_docs, key_docs, head_count, score_scale):
    query_len = query_seq.shape[0]
    key_len = keys_seq.shape[0]
    query_heads = query_seq.reshape(query_len, head_count, -1)
    key_heads = keys_seq.reshape(key_len, head_count, -1)
    scores = (
        jnp.einsum("qhd,khd->hqk", query_heads, key_heads, preferred_element_type=jnp.float32)
        * score_scale
    )
    linked = query_docs[:, None] == key_docs[None, :]
    return jnp.where(linked[None], scores, MASKED)


def score_grads(
    query_seq,
    keys_seq,
    values_seq,
    query_docs,
    key_docs,
    log_seq,
    grad_seq,
    row_sums,
    head_count,
    score_scale,
):
    scores = head_scores(query_seq, keys_seq, query_docs, key_docs, head_count, score_scale)
    prob_rows = jnp.exp(scores - log_seq[..., None])
    value_heads = values_seq.reshape(values_seq.shape[0], head_count, -1)
    grad_heads = grad_seq.reshape(grad_seq.shape[0], head_count, -1)
    prob_grad = jnp.einsum(
        "qhd,khd->hqk", grad_heads, value_heads, preferred_element_type=jnp.float32
    )
    row_sums = jnp.sum(prob_rows * prob_grad, axis=-1)
    score_grad = (prob_rows * (prob_grad - row_sums[..., None])).astype(jnp.bfloat16)
    return (prob_rows, score_grad, row_sums, grad_heads)


def depthwise(padded, kernel, ext_docs, own_docs, halo_reach, local_len):
    tap_count = kernel.shape[0]
    first_tap = halo_reach - tap_count // 2
    result = jnp.zeros(own_docs.shape + (padded.shape[2],), jnp.float32)
    for offset in range(tap_count):
        begin = first_tap + offset
        linked = ext_docs[:, begin : begin + local_len] == own_docs
        shifted = padded[:, begin : begin + local_len].astype(jnp.float32)
        result = result + jnp.where(linked[:, :, None], shifted, 0.0) * kernel[offset].astype(
            jnp.float32
        )
    return result


def depthwise_back(padded, grad_pad, kernel, ext_docs, own_docs, halo_reach, local_len):
    tap_count = kernel.shape[0]
    half_taps = tap_count // 2
    own_grad = grad_pad[:, halo_reach : halo_reach + local_len].astype(jnp.float32)
    back_part = jnp.zeros(own_grad.shape, jnp.float32)
    kernel_rows = []
    for offset in range(tap_count):
        begin = halo_reach - half_taps + offset
        linked = (ext_docs[:, begin : begin + local_len] == own_docs)[:, :, None]
        shifted = padded[:, begin : begin + local_len].astype(jnp.float32)
        kernel_rows.append(jnp.sum(jnp.where(linked, shifted * own_grad, 0.0), axis=(0, 1)))
        mirror = halo_reach + half_taps - offset
        linked_back = (ext_docs[:, mirror : mirror + local_len] == own_docs)[:, :, None]
        mirrored = grad_pad[:, mirror : mirror + local_len].astype(jnp.float32)
        back_part = back_part + jnp.where(linked_back, mirrored, 0.0) * kernel[offset].astype(
            jnp.float32
        )
    return (back_part, jnp.stack(kernel_rows))


def local(
    tokens,
    cotangent,
    path_masks,
    seg_starts,
    query_weight,
    key_weight,
    value_weight,
    output_weight,
    small_kernel,
    middle_kernel,
    large_kernel,
    small_mixer,
    middle_mixer,
    large_mixer,
    inner_weight,
    outer_weight,
    norm_gain,
    norm_bias,
):
    seq_count, local_len, model_dim = tokens.shape
    head_count = model_dim // HD
    score_scale = HD ** (-0.5)
    halo_reach = large_kernel.shape[0] // 2
    seq_len = local_len * lax.axis_size("seq")
    offset_start = lax.axis_index("seq") * local_len
    ext_positions = (
        offset_start - halo_reach + jnp.arange(local_len + 2 * halo_reach, dtype=jnp.int32)
    )
    ext_docs = document_ids(seg_starts, ext_positions, seq_len)
    own_docs = ext_docs[:, halo_reach : halo_reach + local_len]
    key_docs = document_ids(seg_starts, jnp.arange(seq_len, dtype=jnp.int32), seq_len)
    mask_values = path_masks.astype(jnp.float32)
    row_count = seq_count * local_len
    token_rows = tokens.reshape(row_count, model_dim)
    map_batch = max(1, min(seq_count, 512 // local_len))
    query_rows = (
        matmul(token_rows, query_weight)
        .astype(jnp.bfloat16)
        .reshape(seq_count, local_len, model_dim)
    )
    keys_own = (
        matmul(token_rows, key_weight).astype(jnp.bfloat16).reshape(seq_count, local_len, model_dim)
    )
    values_own = (
        matmul(token_rows, value_weight)
        .astype(jnp.bfloat16)
        .reshape(seq_count, local_len, model_dim)
    )
    keys_all, values_all = (
        lax.all_gather(keys_own, "seq", axis=1, tiled=True),
        lax.all_gather(values_own, "seq", axis=1, tiled=True),
    )

    def attend(pieces):
        query_seq, keys_seq, values_seq, query_docs, seq_keys_docs = pieces
        scores = head_scores(
            query_seq, keys_seq, query_docs, seq_keys_docs, head_count, score_scale
        )
        row_top = jnp.max(scores, axis=-1, keepdims=True)
        row_totals = jnp.sum(jnp.exp(scores - row_top), axis=-1, keepdims=True)
        log_totals = row_top + jnp.log(row_totals)
        prob_rows = jnp.exp(scores - log_totals).astype(jnp.bfloat16)
        value_heads = values_seq.reshape(seq_len, head_count, -1)
        attended_seq = jnp.einsum(
            "hqk,khd->qhd", prob_rows, value_heads, preferred_element_type=jnp.float32
        )
        return (attended_seq.reshape(local_len, model_dim), log_totals[..., 0])

    attended, log_sums = lax.map(
        attend, (query_rows, keys_all, values_all, own_docs, key_docs), batch_size=map_batch
    )
    attended_low = attended.astype(jnp.bfloat16).reshape(row_count, model_dim)
    branches = [matmul(attended_low, output_weight)]
    padded = extended(tokens, (("seq", 1),), halo_reach)
    kernels = (small_kernel, middle_kernel, large_kernel)
    mixers = (small_mixer, middle_mixer, large_mixer)
    conv_lows = []
    for kernel, mixer_weight in zip(kernels, mixers):
        conv_low = depthwise(padded, kernel, ext_docs, own_docs, halo_reach, local_len).astype(
            jnp.bfloat16
        )
        conv_low = conv_low.reshape(row_count, model_dim)
        conv_lows.append(conv_low)
        branches.append(matmul(conv_low, mixer_weight))
    hidden = matmul(token_rows, inner_weight)
    activated = gelu_exact(hidden).astype(jnp.bfloat16)
    branches.append(matmul(activated, outer_weight))
    summed = tokens.astype(jnp.float32)
    for position in range(len(branches)):
        summed = summed + mask_values[:, position][:, None, None] * branches[position].reshape(
            seq_count, local_len, model_dim
        )
    centre = jnp.mean(summed, axis=-1, keepdims=True)
    centred = summed - centre
    spread = jnp.mean(centred * centred, axis=-1, keepdims=True)
    inverse = lax.rsqrt(spread + EPSILON)
    normed = centred * inverse
    gain_full = norm_gain.astype(jnp.float32)
    block_output = (normed * gain_full + norm_bias.astype(jnp.float32)).astype(jnp.bfloat16)
    upstream = cotangent.astype(jnp.float32)
    gain_sum = jnp.sum(upstream * normed, axis=(0, 1))
    bias_sum = jnp.sum(upstream, axis=(0, 1))
    scaled_up = upstream * gain_full
    summed_grad = inverse * (
        scaled_up
        - jnp.mean(scaled_up, axis=-1, keepdims=True)
        - normed * jnp.mean(scaled_up * normed, axis=-1, keepdims=True)
    )
    low_grad = summed_grad.astype(jnp.bfloat16)

    def branch_grad(position):
        picked = path_masks[:, position].astype(jnp.bfloat16)[:, None, None]
        return (low_grad * picked).reshape(row_count, model_dim)

    ffn_up = branch_grad(4)
    outer_sum = matmul_tn(activated, ffn_up)
    act_grad = matmul_nt(ffn_up, outer_weight).astype(jnp.bfloat16)
    _, gelu_pull = jax.vjp(gelu_exact, hidden)
    hidden_grad = gelu_pull(act_grad.astype(jnp.float32))[0].astype(jnp.bfloat16)
    inner_sum = matmul_tn(token_rows, hidden_grad)
    input_total = summed_grad.reshape(row_count, model_dim) + matmul_nt(hidden_grad, inner_weight)
    mixer_sums = []
    conv_grads = []
    for position in range(3):
        branch_up = branch_grad(position + 1)
        mixer_sums.append(matmul_tn(conv_lows[position], branch_up))
        conv_grad = matmul_nt(branch_up, mixers[position]).astype(jnp.bfloat16)
        conv_grads.append(conv_grad.reshape(seq_count, local_len, model_dim))
    rim_padded = (
        extended(conv_grads[0], (("seq", 1),), halo_reach),
        extended(conv_grads[1], (("seq", 1),), halo_reach),
        extended(conv_grads[2], (("seq", 1),), halo_reach),
    )
    kernel_sums = []
    for position in range(3):
        back_part, kernel_part = depthwise_back(
            padded,
            rim_padded[position],
            kernels[position],
            ext_docs,
            own_docs,
            halo_reach,
            local_len,
        )
        input_total = input_total + back_part.reshape(row_count, model_dim)
        kernel_sums.append(kernel_part)
    attn_up = branch_grad(0)
    output_sum = matmul_tn(attended_low, attn_up)
    attended_grad = (
        matmul_nt(attn_up, output_weight)
        .astype(jnp.bfloat16)
        .reshape(seq_count, local_len, model_dim)
    )
    keys_back, values_back = (keys_all, values_all)

    def attend_back(pieces):
        query_seq, keys_seq, values_seq, query_docs, seq_keys_docs, log_seq, grad_seq = pieces
        prob_rows, score_grad, row_sums, grad_heads = score_grads(
            query_seq,
            keys_seq,
            values_seq,
            query_docs,
            seq_keys_docs,
            log_seq,
            grad_seq,
            None,
            head_count,
            score_scale,
        )
        key_heads = keys_seq.reshape(seq_len, head_count, -1)
        query_heads = query_seq.reshape(local_len, head_count, -1)
        query_part = (
            jnp.einsum("hqk,khd->qhd", score_grad, key_heads, preferred_element_type=jnp.float32)
            * score_scale
        )
        key_part = (
            jnp.einsum("hqk,qhd->khd", score_grad, query_heads, preferred_element_type=jnp.float32)
            * score_scale
        )
        value_part = jnp.einsum(
            "hqk,qhd->khd",
            prob_rows.astype(jnp.bfloat16),
            grad_heads,
            preferred_element_type=jnp.float32,
        )
        return (
            query_part.reshape(local_len, model_dim),
            key_part.reshape(seq_len, model_dim),
            value_part.reshape(seq_len, model_dim),
        )

    query_parts, key_parts, value_parts = lax.map(
        attend_back,
        (query_rows, keys_back, values_back, own_docs, key_docs, log_sums, attended_grad),
        batch_size=map_batch,
    )
    key_total, value_total = (
        lax.psum_scatter(key_parts, "seq", scatter_dimension=1, tiled=True),
        lax.psum_scatter(value_parts, "seq", scatter_dimension=1, tiled=True),
    )
    query_act = query_parts.astype(jnp.bfloat16).reshape(row_count, model_dim)
    key_act = key_total.astype(jnp.bfloat16).reshape(row_count, model_dim)
    value_act = value_total.astype(jnp.bfloat16).reshape(row_count, model_dim)
    query_sum = matmul_tn(token_rows, query_act)
    key_sum = matmul_tn(token_rows, key_act)
    value_sum = matmul_tn(token_rows, value_act)
    input_total = (
        input_total
        + matmul_nt(query_act, query_weight)
        + matmul_nt(key_act, key_weight)
        + matmul_nt(value_act, value_weight)
    )
    input_grad = input_total.astype(jnp.bfloat16).reshape(seq_count, local_len, model_dim)
    op_counts = lax.psum(jnp.sum(path_masks, axis=0), "batch").astype(jnp.float32)
    shares = (
        lax.psum_scatter(query_sum, "batch", scatter_dimension=0, tiled=True),
        lax.psum_scatter(key_sum, "batch", scatter_dimension=0, tiled=True),
        lax.psum_scatter(value_sum, "batch", scatter_dimension=0, tiled=True),
        lax.psum_scatter(output_sum, "batch", scatter_dimension=0, tiled=True),
        lax.psum_scatter(kernel_sums[0].T, "batch", scatter_dimension=0, tiled=True),
        lax.psum_scatter(kernel_sums[1].T, "batch", scatter_dimension=0, tiled=True),
        lax.psum_scatter(kernel_sums[2].T, "batch", scatter_dimension=0, tiled=True),
        lax.psum_scatter(mixer_sums[0], "batch", scatter_dimension=0, tiled=True),
        lax.psum_scatter(mixer_sums[1], "batch", scatter_dimension=0, tiled=True),
        lax.psum_scatter(mixer_sums[2], "batch", scatter_dimension=0, tiled=True),
        lax.psum_scatter(inner_sum, "batch", scatter_dimension=0, tiled=True),
        lax.psum_scatter(outer_sum, "batch", scatter_dimension=0, tiled=True),
        lax.psum_scatter(gain_sum, "batch", scatter_dimension=0, tiled=True),
        lax.psum_scatter(bias_sum, "batch", scatter_dimension=0, tiled=True),
    )
    reduced = lax.psum(
        (
            shares[0],
            shares[1],
            shares[2],
            shares[3],
            shares[4],
            shares[5],
            shares[6],
            shares[7],
            shares[8],
            shares[9],
            shares[10],
            shares[11],
            shares[12],
            shares[13],
        ),
        "seq",
    )
    return (
        block_output,
        input_grad,
        reduced[0] / op_counts[0],
        reduced[1] / op_counts[0],
        reduced[2] / op_counts[0],
        reduced[3] / op_counts[0],
        (reduced[4] / op_counts[1]).T,
        (reduced[5] / op_counts[2]).T,
        (reduced[6] / op_counts[3]).T,
        reduced[7] / op_counts[1],
        reduced[8] / op_counts[2],
        reduced[9] / op_counts[3],
        reduced[10] / op_counts[4],
        reduced[11] / op_counts[4],
        reduced[12],
        reduced[13],
    )


def solution(mesh):
    in_specs = (
        P("batch", "seq", None),
        P("batch", "seq", None),
        P("batch", None),
        P("batch", None),
        P(),
        P(),
        P(),
        P(),
        P(),
        P(),
        P(),
        P(),
        P(),
        P(),
        P(),
        P(),
        P(),
        P(),
    )
    out_specs = (
        P("batch", "seq", None),
        P("batch", "seq", None),
        P("batch", None),
        P("batch", None),
        P("batch", None),
        P("batch", None),
        P(None, "batch"),
        P(None, "batch"),
        P(None, "batch"),
        P("batch", None),
        P("batch", None),
        P("batch", None),
        P("batch", None),
        P("batch", None),
        P("batch"),
        P("batch"),
    )
    return jax.shard_map(local, mesh=mesh, in_specs=in_specs, out_specs=out_specs, check_vma=False)
```

profile of v0, /device:TPU:0, one launch (start us, length us, event | category | flops | bytes accessed | tf_op | source)
XLA Modules:
  0.0 1361.3 jit_solution(9327208576023645812)
XLA Ops:
  7.3 3.0 convolution_convert_fusion.6
  11.7 3.0 collective-permute-start
  14.7 2.7 convolution_convert_fusion.8
  18.3 14.8 %multiply_convert_fusion.1 = (bf16[384,3072]{1,0:T(8,128)(2,1)S(1)}, f32[384,3072]{1,0:T(8,128)}, f32[384,3072]{1,0:T(8,128)}) fusion(bf16[384,768]{1,0:T(8,128)(2,1)S(1)} %bitcast.162, bf16[768,3072]{1,0:T(8,128)(2,1)} %param.32), kind=kOutput, calls=%fused_computation.19 | convolution fusion | flops 1888616448 | bytes 17104896 | tf_op jit(solution)/shard_map/dot_general | solution.py:34
  34.6 5.4 fusion.126
  42.2 2.2 copy.99
  44.4 2.5 fusion.41
  48.0 2.3 fusion.38
  50.3 4.3 copy.98
  54.6 3.7 fusion
  58.3 2.6 exponential_reduce_fusion
  63.5 4.7 copy.96
  68.3 7.1 convolution_convert_fusion.5
  90.5 8.5 fusion.108
  98.9 6.1 copy.107
  105.1 6.8 multiply_reduce_fusion
  111.9 6.4 multiply_convert_fusion
  118.3 3.5 broadcast_multiply_fusion
  122.1 6.1 copy.105
  129.2 3.3 convolution_bitcast_fusion.4
  132.6 4.8 fusion.35
  137.4 2.2 convolution_bitcast_fusion.7
  139.7 3.1 copy.127
  142.8 11.4 reduce-scatter.33.cloned.1.call-done
  156.4 2.2 convolution_bitcast_fusion.5
  158.6 3.1 copy.131
  161.8 42.9 %reduce-scatter.31.cloned.1.call-done = f32[3,128,768]{2,1,0:T(8,128)} async-done(((f32[3,512,768]{2,1,0:T(8,128)}), f32[3,128,768]{2,1,0:T(8,128)}) %reduce-scatter.31.cloned.1.call-update) | async-done | bytes 1179664 | tf_op jit(solution)/shard_map/reduce_scatter | solution.py:322
  206.9 2.2 convolution_bitcast_fusion.6
  209.1 3.1 copy.129
  212.2 2.4 broadcast_multiply_fusion.5
  214.6 7.8 fusion.7
  223.8 5.1 convolution_bitcast_fusion
  229.0 9.7 copy.141
  239.0 3.4 convolution_bitcast_fusion.1
  242.5 3.5 convolution_bitcast_fusion.2
  246.1 3.5 convolution_bitcast_fusion.3
  249.6 8.1 fusion.127
  257.8 11.5 psum.106
  271.1 2.2 convolution_convert_fusion.4
  276.0 3.4 fusion.87
  283.4 3.0 collective-permute-start.7
  287.6 19.6 %all-reduce.2 = (f32[768]{0:T(1024)S(1)}, f32[768]{0:T(1024)S(1)}) all-reduce(f32[768]{0:T(1024)S(1)} %get-tuple-element.137, f32[768]{0:T(1024)S(1)} %get-tuple-element.173), channel_id=16, replica_groups=mesh['batch'=8,'seq'=4] {'batch'}, use_global_device_ids=true, to_apply=%region_53.54.clone | all-reduce | flops 1536 | bytes 12288
  308.6 3.0 collective-permute-start.3
  315.5 3.3 collective-permute-start.5
  318.8 2.6 fusion.80
  321.4 2.5 fusion.66
  327.5 21.6 %reduce-scatter.43.cloned.1.call-done = f32[96,768]{1,0:T(8,128)} async-done(((f32[768,768]{1,0:T(8,128)}), f32[96,768]{1,0:T(8,128)}) %reduce-scatter.43.cloned.1.call-update) | async-done | bytes 294928
  351.0 69.7 %reduce-scatter.47.cloned.1.call-done = f32[96,768]{1,0:T(8,128)} async-done(((f32[768,768]{1,0:T(8,128)}), f32[96,768]{1,0:T(8,128)}) %reduce-scatter.47.cloned.1.call-update) | async-done | bytes 294928
  422.6 69.7 %reduce-scatter.45.cloned.1.call-done = f32[96,768]{1,0:T(8,128)} async-done(((f32[768,768]{1,0:T(8,128)}), f32[96,768]{1,0:T(8,128)}) %reduce-scatter.45.cloned.1.call-update) | async-done | bytes 294928
  494.2 164.3 %reduce-scatter.57.cloned.1.call-done = f32[96,3072]{1,0:T(8,128)} async-done(((f32[768,3072]{1,0:T(8,128)}), f32[96,3072]{1,0:T(8,128)}) %reduce-scatter.57.cloned.1.call-update) | async-done | bytes 1179664
  658.5 2.9 copy.142
  661.4 68.6 %reduce-scatter.39.cloned.1.call-done = f32[96,768]{1,0:T(8,128)} async-done(((f32[768,768]{1,0:T(8,128)}), f32[96,768]{1,0:T(8,128)}) %reduce-scatter.39.cloned.1.call-update) | async-done | bytes 294928 | tf_op jit(solution)/shard_map/reduce_scatter | solution.py:349
  729.9 71.6 %reduce-scatter.37.cloned.1.call-done = f32[96,768]{1,0:T(8,128)} async-done(((f32[768,768]{1,0:T(8,128)}), f32[96,768]{1,0:T(8,128)}) %reduce-scatter.37.cloned.1.call-update) | async-done | bytes 294928 | tf_op jit(solution)/shard_map/reduce_scatter | solution.py:348
  801.6 71.4 %reduce-scatter.35.cloned.1.call-done = f32[96,768]{1,0:T(8,128)} async-done(((f32[768,768]{1,0:T(8,128)}), f32[96,768]{1,0:T(8,128)}) %reduce-scatter.35.cloned.1.call-update) | async-done | bytes 294928 | tf_op jit(solution)/shard_map/reduce_scatter | solution.py:347
  873.0 166.1 %reduce-scatter.41.cloned.1.call-done = f32[384,768]{1,0:T(8,128)} async-done(((f32[3072,768]{1,0:T(8,128)}), f32[384,768]{1,0:T(8,128)}) %reduce-scatter.41.cloned.1.call-update) | async-done | bytes 1179664 | tf_op jit(solution)/shard_map/reduce_scatter | solution.py:351
  1040.4 6.2 fusion.34
  1048.4 54.4 %reduce-scatter.51.cloned.1.call-done = f32[96,3]{1,0:T(8,128)} async-done(((f32[768,3]{1,0:T(8,128)}), f32[96,3]{1,0:T(8,128)}) %reduce-scatter.51.cloned.1.call-update) | async-done | bytes 1168
  1103.7 62.7 %reduce-scatter.53.cloned.1.call-done = f32[96,5]{1,0:T(8,128)} async-done(((f32[768,5]{1,0:T(8,128)}), f32[96,5]{1,0:T(8,128)}) %reduce-scatter.53.cloned.1.call-update) | async-done | bytes 1936
  1167.2 62.7 %reduce-scatter.55.cloned.1.call-done = f32[96,7]{1,0:T(8,128)} async-done(((f32[768,7]{1,0:T(8,128)}), f32[96,7]{1,0:T(8,128)}) %reduce-scatter.55.cloned.1.call-update) | async-done | bytes 2704
  1230.8 11.1 all-reduce.3
  1245.6 2.4 convolution_add_fusion.1
  1249.5 85.9 %all-reduce.7.cloned.1.call-done = (f32[96,768]{0,1:T(8,128)}, f32[96,768]{0,1:T(8,128)}, f32[96,768]{0,1:T(8,128)}, f32[96,768]{0,1:T(8,128)}, f32[96,768]{1,0:...) async-done(((f32[96,768]{0,1:T(8,128)}, f32[96,768]{0,1:T(8,128)}, f32[96,768]{0,1:T(8,128)}, f32[96,768]{0,1:T(8,128)}, ...) | async-done | bytes 4423696 | tf_op jit(solution)/shard_map/psum | solution.py:355
  1346.6 3.1 broadcast_divide_fusion.1
  1351.5 2.9 copy.118
  (259 shorter events, 79.2 us)
Async XLA Ops:
  7.2 71.9 %copy-start = (bf16[768,768]{1,0:T(8,128)(2,1)S(1)}, bf16[768,768]{1,0:T(8,128)(2,1)}, u32[]{:S(2)}) copy-start(bf16[768,768]{1,0:T(8,128)(2,1)} %param.31) | copy-start | bytes 3538948
  7.2 43.1 %all-gather.5.cloned.1.call-start = ((), (), s32[]{:S(2)}) async-start(), calls=%async_computation.15 | async-start | bytes 2949120 | tf_op jit(solution)/shard_map/all_gather | solution.py:174
  7.2 3.1 copy-start.3
  10.3 53.2 %all-gather.3.cloned.1.call-start = ((), (), s32[]{:S(2)}) async-start(), calls=%async_computation.14 | async-start | bytes 2949120 | tf_op jit(solution)/shard_map/all_gather | solution.py:175
  10.4 34.0 %collective-permute-start.1 = (bf16[3,3,768]{2,1,0:T(4,128)(2,1)S(1)}, bf16[3,3,768]{2,1,0:T(4,128)(2,1)S(1)}, u32[]{:S(2)}, u32[]{:S(2)}) collective-permute-start(bf16[3,3,768]{2,1,0:T(4,128)(2,1)S(1)} %get-tuple-element.249), channel_id=1, source_target_pairs={{1,0},{2,1},{3,2},{5,4},{6,5},{7,6},{9,8},{10,9},{11,10},{13,12},{... | collective-permute-start | bytes 41480 | tf_op jit(solution)/shard_map/ppermute | solution.py:21
  11.7 5.9 copy-start.52
  11.7 32.7 %collective-permute-start = (bf16[3,3,768]{2,1,0:T(4,128)(2,1)S(1)}, bf16[3,3,768]{2,1,0:T(4,128)(2,1)S(1)}, u32[]{:S(2)}, u32[]{:S(2)}) collective-permute-start(bf16[3,3,768]{2,1,0:T(4,128)(2,1)S(1)} %get-tuple-element.250), channel_id=1, source_target_pairs={{0,1},{1,2},{2,3},{4,5},{5,6},{6,7},{8,9},{9,10},{10,11},{12,13},{... | collective-permute-start | bytes 41480 | tf_op jit(solution)/shard_map/ppermute | solution.py:20
  17.5 136.8 %reduce-scatter.33.cloned.1.call-start = ((), (), s32[]{:S(2)}) async-start(), calls=%async_computation.17 | async-start | bytes 5898240 | tf_op jit(solution)/shard_map/reduce_scatter | solution.py:323
  18.2 14.9 %copy-start.50 = (bf16[5,768]{1,0:T(8,128)(2,1)S(1)}, bf16[5,768]{1,0:T(8,128)(2,1)}, u32[]{:S(2)}) copy-start(bf16[5,768]{1,0:T(8,128)(2,1)} %param.27) | copy-start | bytes 23044
  18.2 14.9 %copy-start.51 = (bf16[3,768]{1,0:T(4,128)(2,1)S(1)}, bf16[3,768]{1,0:T(4,128)(2,1)}, u32[]{:S(2)}) copy-start(bf16[3,768]{1,0:T(4,128)(2,1)} %param.26) | copy-start | bytes 13828
  18.3 15.4 %copy-start.40 = (bf16[768,768]{1,0:T(8,128)(2,1)S(1)}, bf16[768,768]{1,0:T(8,128)(2,1)}, u32[]{:S(2)}) copy-start(bf16[768,768]{1,0:T(8,128)(2,1)} %param.22) | copy-start | bytes 3538948
  33.1 1.5 copy-start.18
  34.6 5.6 copy-start.53
  34.6 5.7 copy-start.54
  44.3 10.3 copy-start.4
  58.3 3.6 copy-start.1
  68.3 7.1 copy-start.36
  75.4 1.7 copy-start.37
  77.0 1.5 copy-start.38
  78.5 1.5 copy-start.42
  105.1 99.6 %reduce-scatter.31.cloned.1.call-start = ((), (), s32[]{:S(2)}) async-start(), calls=%async_computation.16 | async-start | bytes 5898240 | tf_op jit(solution)/shard_map/reduce_scatter | solution.py:322
  111.9 6.4 copy-start.5
  118.3 3.8 copy-start.2
  128.2 197.4 %reduce-scatter.49.cloned.1.call-start = ((), (), s32[]{:S(2)}) async-start(), calls=%async_computation.25 | async-start | bytes 2654208
  132.6 216.5 %reduce-scatter.43.cloned.1.call-start = ((), (), s32[]{:S(2)}) async-start(), calls=%async_computation.22 | async-start | bytes 2654208
  142.8 278.0 %reduce-scatter.47.cloned.1.call-start = ((), (), s32[]{:S(2)}) async-start(), calls=%async_computation.24 | async-start | bytes 2654208
  161.8 330.5 %reduce-scatter.45.cloned.1.call-start = ((), (), s32[]{:S(2)}) async-start(), calls=%async_computation.23 | async-start | bytes 2654208
  212.2 446.3 %reduce-scatter.57.cloned.1.call-start = ((), (), s32[]{:S(2)}) async-start(), calls=%async_computation.29 | async-start | bytes 10616832
  214.6 7.8 copy-start.26
  222.4 1.4 copy-start.17
  238.7 491.2 %reduce-scatter.39.cloned.1.call-start = ((), (), s32[]{:S(2)}) async-start(), calls=%async_computation.20 | async-start | bytes 2654208 | tf_op jit(solution)/shard_map/reduce_scatter | solution.py:349
  242.5 559.1 %reduce-scatter.37.cloned.1.call-start = ((), (), s32[]{:S(2)}) async-start(), calls=%async_computation.19 | async-start | bytes 2654208 | tf_op jit(solution)/shard_map/reduce_scatter | solution.py:348
  246.0 627.0 %reduce-scatter.35.cloned.1.call-start = ((), (), s32[]{:S(2)}) async-start(), calls=%async_computation.18 | async-start | bytes 2654208 | tf_op jit(solution)/shard_map/reduce_scatter | solution.py:347
  249.6 789.6 %reduce-scatter.41.cloned.1.call-start = ((), (), s32[]{:S(2)}) async-start(), calls=%async_computation.21 | async-start | bytes 10616832 | tf_op jit(solution)/shard_map/reduce_scatter | solution.py:351
  257.7 11.6 copy-start.56
  257.8 845.1 %reduce-scatter.51.cloned.1.call-start = ((), (), s32[]{:S(2)}) async-start(), calls=%async_computation.26 | async-start | bytes 442368
  271.1 2.3 copy-start.31
  271.1 2.3 copy-start.39
  273.4 2.0 copy-start.19
  275.4 4.0 copy-start.23
  279.3 8.2 copy-start.22
  281.2 885.2 %reduce-scatter.53.cloned.1.call-start = ((), (), s32[]{:S(2)}) async-start(), calls=%async_computation.27 | async-start | bytes 442368
  282.1 33.3 %collective-permute-start.6 = (bf16[3,3,768]{2,1,0:T(4,128)(2,1)S(1)}, bf16[3,3,768]{2,1,0:T(4,128)(2,1)S(1)}, u32[]{:S(2)}, u32[]{:S(2)}) collective-permute-start(bf16[3,3,768]{2,1,0:T(4,128)(2,1)S(1)} %get-tuple-element.247), channel_id=1, source_target_pairs={{1,0},{2,1},{3,2},{5,4},{6,5},{7,6},{9,8},{10,9},{11,10},{13,12},{... | collective-permute-start | bytes 41480 | tf_op jit(solution)/shard_map/ppermute | solution.py:21
  283.4 35.3 %collective-permute-start.7 = (bf16[3,3,768]{2,1,0:T(4,128)(2,1)S(1)}, bf16[3,3,768]{2,1,0:T(4,128)(2,1)S(1)}, u32[]{:S(2)}, u32[]{:S(2)}) collective-permute-start(bf16[3,3,768]{2,1,0:T(4,128)(2,1)S(1)} %get-tuple-element.248), channel_id=1, source_target_pairs={{0,1},{1,2},{2,3},{4,5},{5,6},{6,7},{8,9},{9,10},{10,11},{12,13},{... | collective-permute-start | bytes 41480 | tf_op jit(solution)/shard_map/ppermute | solution.py:20
  287.5 942.5 %reduce-scatter.55.cloned.1.call-start = ((), (), s32[]{:S(2)}) async-start(), calls=%async_computation.28 | async-start | bytes 442368
  287.5 31.2 %copy-start.24 = (bf16[384,768]{1,0:T(8,128)(2,1)S(1)}, bf16[384,768]{1,0:T(8,128)(2,1)}, u32[]{:S(2)}) copy-start(bf16[384,768]{1,0:T(8,128)(2,1)} %copy-done.23) | copy-start | bytes 1769476
  307.3 16.6 %collective-permute-start.2 = (bf16[3,3,768]{2,1,0:T(4,128)(2,1)S(1)}, bf16[3,3,768]{2,1,0:T(4,128)(2,1)S(1)}, u32[]{:S(2)}, u32[]{:S(2)}) collective-permute-start(bf16[3,3,768]{2,1,0:T(4,128)(2,1)S(1)} %get-tuple-element.243), channel_id=1, source_target_pairs={{1,0},{2,1},{3,2},{5,4},{6,5},{7,6},{9,8},{10,9},{11,10},{13,12},{... | collective-permute-start | bytes 41480 | tf_op jit(solution)/shard_map/ppermute | solution.py:21
  308.6 15.4 %collective-permute-start.3 = (bf16[3,3,768]{2,1,0:T(4,128)(2,1)S(1)}, bf16[3,3,768]{2,1,0:T(4,128)(2,1)S(1)}, u32[]{:S(2)}, u32[]{:S(2)}) collective-permute-start(bf16[3,3,768]{2,1,0:T(4,128)(2,1)S(1)} %get-tuple-element.244), channel_id=1, source_target_pairs={{0,1},{1,2},{2,3},{4,5},{5,6},{6,7},{8,9},{9,10},{10,11},{12,13},{... | collective-permute-start | bytes 41480 | tf_op jit(solution)/shard_map/ppermute | solution.py:20
  311.6 9.8 collective-permute-start.4
  315.4 1020.0 %all-reduce.7.cloned.1.call-start = ((), (), s32[]{:S(2)}) async-start(), calls=%async_computation.30 | async-start | bytes 10420224 | tf_op jit(solution)/shard_map/psum | solution.py:355
  315.5 6.0 collective-permute-start.5
  321.4 2.5 copy-start.20
  1040.4 6.3 copy-start.25
  1040.4 6.3 copy-start.41
  1046.7 198.9 %copy-start.16 = (bf16[3,128,768]{2,1,0:T(8,128)(2,1)S(1)}, bf16[3,128,768]{2,1,0:T(8,128)(2,1)}, u32[]{:S(2)}) copy-start(bf16[3,128,768]{2,1,0:T(8,128)(2,1)} %copy-done.15) | copy-start | bytes 1769476
  1245.6 2.4 copy-start.11
  1245.6 2.4 copy-start.34
  1335.4 2.6 copy-start.48
  1335.4 3.9 copy-start.47
  1335.4 5.3 copy-start.46
  1337.1 5.1 copy-start.45
  1340.7 2.9 copy-start.44
  1342.8 2.4 copy-start.43
  1346.6 3.1 copy-start.33
  (18 other events, 18.4 us)
Sparse Core Ops, SparseCore 0:
  10.4 26.7 all-gather.4
  39.4 24.1 all-gather.2
  105.2 49.0 reduce-scatter.32
  156.8 47.8 reduce-scatter.30
  208.0 69.2 reduce-scatter.48
  280.6 68.4 reduce-scatter.42
  352.6 68.0 reduce-scatter.46
  424.2 68.0 reduce-scatter.44
  495.9 162.5 reduce-scatter.56
  661.8 68.0 reduce-scatter.38
  733.4 68.0 reduce-scatter.36
  804.9 68.0 reduce-scatter.34
  876.6 162.5 reduce-scatter.40
  1042.3 60.4 reduce-scatter.50
  1105.9 60.4 reduce-scatter.52
  1169.5 60.3 reduce-scatter.54
  1232.8 102.5 all-reduce.6
where the time goes:
time: 1370 us; the launch traced here: 1360 us
  waiting for transfers between devices  1030 us (75%)
  matrix products  121 us (9%)
  local copies, waits for them, and re-layouts  89.3 us (7%)
  other arithmetic  49.4 us (4%)
  blocking collectives  42.1 us (3%)
  starting transfers between devices  18.5 us (1%)
  between operations  16.1 us (1%)
    unnamed x25, waiting for transfers between devices  505 us
    reduce_scatter x1, waiting for transfers between devices, local(): lax.psum_scatter(outer_sum, 'batch', scatter_dimension=0, tiled=True)  166 us
    psum x1, waiting for transfers between devices, local(): lax.psum((shares[0], shares[1], shares[2], shares[3], shares[4], shares[5...  85.9 us
    reduce_scatter x1, waiting for transfers between devices, local(): lax.psum_scatter(mixer_sums[1], 'batch', scatter_dimension=0, tiled=True)  71.6 us
    reduce_scatter x1, waiting for transfers between devices, local(): lax.psum_scatter(mixer_sums[0], 'batch', scatter_dimension=0, tiled=True)  71.4 us
    reduce_scatter x1, waiting for transfers between devices, local(): lax.psum_scatter(mixer_sums[2], 'batch', scatter_dimension=0, tiled=True)  68.6 us
    unnamed x138, local copies, waits for them, and re-layouts  55.7 us
    reduce_scatter x1, waiting for transfers between devices, local(): lax.psum_scatter(key_parts, 'seq', scatter_dimension=1, tiled=True)  42.9 us
  transfers between devices with their start and end apart: 25, of which 15 were waited for; matrix products, arithmetic and copies ran while one was open for 14% of the time, Pallas kernels for 0%

commit v1 on v0

v1 whole, which is shorter than its diff:
```python
import functools

import jax
import jax.numpy as jnp
from jax import lax
from jax.experimental import pallas as pl
from jax.experimental.pallas import tpu as pltpu
from jax.sharding import PartitionSpec as P

HD = 64
EPSILON = 1e-05
MASKED = -1e30
TAPS = (3, 5, 7)
F32 = jnp.float32
BF16 = jnp.bfloat16
VMEM_LIMIT = 56 * 1024 * 1024


def dot_nn(left, right):
    return jnp.dot(left, right, preferred_element_type=F32)


def dot_nt(left, right):
    return lax.dot_general(left, right, (((1,), (1,)), ((), ())), preferred_element_type=F32)


def dot_tn(left, right):
    return lax.dot_general(left, right, (((0,), (0,)), ((), ())), preferred_element_type=F32)


def doc_of(starts_ref, row, positions):
    found = jnp.zeros(positions.shape, jnp.int32)
    for which in range(starts_ref.shape[1]):
        found = found + (starts_ref[row, which] <= positions).astype(jnp.int32)
    return found


def assemble(full_ref, pieces, g, rows):
    for k, piece in enumerate(pieces):
        full_ref[0, pl.ds(pl.multiple_of((g ^ k) * rows, rows), rows), :] = piece[0]


def channels(out_ref, source, g, count, width, pad):
    length = source.shape[0]
    out_ref[0:pad, :] = jnp.zeros((pad, width), F32)
    out_ref[pad + length : 2 * pad + length, :] = jnp.zeros((pad, width), F32)
    for which in range(count):

        @pl.when(g == which)
        def _():
            out_ref[pad : pad + length, :] = source[:, which * width : (which + 1) * width].astype(F32)


def forward_kernel(
    count, g_ref, masks_ref, starts_ref, t0, t1, t2, t3, wqkv_ref, win_ref, wrow_ref, taps_ref,
    p0, p1, p2, p3, tok_ref, mcat_ref, slope_ref, qkv_ref, probs_ref, scaled_ref, chan_ref, part_ref,
):
    step = pl.program_id(0)
    g = g_ref[0]
    rows = t0.shape[1]
    length = tok_ref.shape[1]
    ffn = win_ref.shape[1]
    width = wqkv_ref.shape[1] // 3
    heads = width // HD
    assemble(tok_ref, (t0, t1, t2, t3), g, rows)
    masks = [masks_ref[step, c].astype(F32) for c in range(5)]

    qkv = dot_nn(tok_ref[0], wqkv_ref[...]).astype(BF16)
    qkv_ref[0, :, 0:width] = qkv[:, 0:width] * jnp.asarray(HD**-0.5, BF16)
    qkv_ref[0, :, width:] = qkv[:, width:]

    key_docs = doc_of(starts_ref, step, lax.broadcasted_iota(jnp.int32, (1, length), 1))
    tile = length // 4
    ones = jnp.ones((length, HD), BF16)
    for h in range(heads):
        keys = qkv_ref[0, :, width + h * HD : width + (h + 1) * HD]
        values = jnp.concatenate([qkv_ref[0, :, 2 * width + h * HD : 2 * width + (h + 1) * HD], ones], axis=1)

        def attend(i, carry, h=h, keys=keys, values=values):
            start = pl.multiple_of(i * tile, tile)
            docs = doc_of(starts_ref, step, start + lax.broadcasted_iota(jnp.int32, (tile, 1), 0))
            scores = dot_nt(qkv_ref[0, pl.ds(start, tile), h * HD : (h + 1) * HD], keys)
            scores = jnp.where(docs == key_docs, scores, MASKED)
            top = jnp.max(scores, axis=1, keepdims=True)
            weights = jnp.exp(scores - top)
            total = jnp.sum(weights, axis=1, keepdims=True)
            low = (weights * (1.0 / total)).astype(BF16)
            probs_ref[0, h, pl.ds(start, tile), :] = low
            both = dot_nn(low, values)
            attended = both[:, 0:HD]
            scaled_ref[0, pl.ds(start, tile), h * HD : (h + 1) * HD] = attended / both[:, HD : 2 * HD]
            mcat_ref[0, pl.ds(start, tile), ffn + h * HD : ffn + (h + 1) * HD] = (
                attended.astype(BF16) * masks[0].astype(BF16)
            )
            return carry

        lax.fori_loop(0, length // tile, attend, 0)

    pad = 8
    channels(chan_ref, tok_ref.at[0], g, count, width, pad)
    for start in range(0, length, 128):
        sums = [jnp.zeros((128, width), F32) for _ in TAPS]
        here = start + lax.broadcasted_iota(jnp.int32, (128, 1), 0)
        docs = doc_of(starts_ref, step, here)
        for shift in range(-3, 4):
            moved = chan_ref[pad + start + shift : pad + start + shift + 128, :]
            if shift != 0:
                moved = jnp.where(docs == doc_of(starts_ref, step, here + shift), moved, 0.0)
            base = 0
            for k, taps in enumerate(TAPS):
                if abs(shift) <= taps // 2:
                    tap = base + shift + taps // 2
                    sums[k] = sums[k] + moved * taps_ref[tap : tap + 1, :]
                base += taps
        for k in range(3):
            lane = ffn + (k + 1) * width
            mcat_ref[0, start : start + 128, lane : lane + width] = (sums[k] * masks[k + 1]).astype(BF16)

    def feed(i, carry):
        start = pl.multiple_of(i * 128, 128)
        hidden = dot_nn(tok_ref[0, pl.ds(start, 128), :], win_ref[...])
        cdf = 0.5 * (1.0 + lax.erf(hidden * (0.5**0.5)))
        density = jnp.exp(-0.5 * hidden * hidden) * 0.3989422804014327
        mcat_ref[0, pl.ds(start, 128), 0:ffn] = (hidden * cdf * masks[4]).astype(BF16)
        slope_ref[0, pl.ds(start, 128), :] = cdf + hidden * density
        return carry

    lax.fori_loop(0, length // 128, feed, 0)

    part_ref[...] = dot_nn(mcat_ref[0], wrow_ref[...])
    for k, out in enumerate((p0, p1, p2, p3)):
        out[0] = part_ref[pl.ds(pl.multiple_of((g ^ k) * rows, rows), rows), :].astype(BF16)


def norm_kernel(tok_ref, a_ref, b_ref, c_ref, cot_ref, gain_ref, bias_ref, out_ref, grad_ref, low_ref, sums_ref):
    step = pl.program_id(0)
    summed = tok_ref[0].astype(F32) + (a_ref[0].astype(F32) + b_ref[0].astype(F32) + c_ref[0].astype(F32))
    centred = summed - jnp.mean(summed, axis=1, keepdims=True)
    inverse = lax.rsqrt(jnp.mean(centred * centred, axis=1, keepdims=True) + EPSILON)
    normed = centred * inverse
    gain = gain_ref[...].astype(F32)
    out_ref[0] = (normed * gain + bias_ref[...].astype(F32)).astype(BF16)
    upstream = cot_ref[0].astype(F32)

    @pl.when(step == 0)
    def _():
        sums_ref[...] = jnp.zeros(sums_ref.shape, F32)

    sums_ref[0:1, :] += jnp.sum(upstream * normed, axis=0, keepdims=True)
    sums_ref[1:2, :] += jnp.sum(upstream, axis=0, keepdims=True)
    scaled = upstream * gain
    grad = inverse * (
        scaled
        - jnp.mean(scaled, axis=1, keepdims=True)
        - normed * jnp.mean(scaled * normed, axis=1, keepdims=True)
    )
    grad_ref[0] = grad
    low_ref[0] = grad.astype(BF16)


def backward_kernel(
    count, g_ref, masks_ref, starts_ref, l0, l1, l2, l3, tok_ref, slope_ref, qkv_ref, probs_ref, scaled_ref,
    wrow_ref, wcat_ref, taps_ref,
    p0, p1, p2, p3, acts_ref, tapsum_ref, low_ref, up_ref, chan_ref, c3_ref, c5_ref, c7_ref, part_ref,
):
    step = pl.program_id(0)
    g = g_ref[0]
    rows = l0.shape[1]
    length = tok_ref.shape[1]
    ffn = slope_ref.shape[2]
    width = qkv_ref.shape[2] // 3
    heads = width // HD
    pad = 8
    assemble(low_ref, (l0, l1, l2, l3), g, rows)
    masks = [masks_ref[step, c].astype(F32) for c in range(5)]

    def feed(i, carry):
        start = pl.multiple_of(i * 128, 128)
        grads = dot_nt(low_ref[0, pl.ds(start, 128), :], wrow_ref[0:ffn, :])
        grads = (grads * masks[4]).astype(BF16).astype(F32)
        acts_ref[0, pl.ds(start, 128), 0:ffn] = (grads * slope_ref[0, pl.ds(start, 128), :]).astype(BF16)
        return carry

    lax.fori_loop(0, length // 128, feed, 0)

    ups = dot_nt(low_ref[0], wrow_ref[ffn:, :])
    up_ref[...] = (ups[:, 0:width] * masks[0]).astype(BF16)
    conv_refs = (c3_ref, c5_ref, c7_ref)
    for k, ref in enumerate(conv_refs):
        ref[0:pad, :] = jnp.zeros((pad, width), F32)
        ref[pad + length : 2 * pad + length, :] = jnp.zeros((pad, width), F32)
        ref[pad : pad + length, :] = (
            (ups[:, (k + 1) * width : (k + 2) * width] * masks[k + 1]).astype(BF16).astype(F32)
        )

    tile = length // 2
    for h in range(heads):
        keys = qkv_ref[0, :, width + h * HD : width + (h + 1) * HD]
        values = qkv_ref[0, :, 2 * width + h * HD : 2 * width + (h + 1) * HD]
        key_sum = jnp.zeros((HD, length), F32)
        value_sum = jnp.zeros((HD, length), F32)
        for start in range(0, length, tile):
            query = qkv_ref[0, start : start + tile, h * HD : (h + 1) * HD]
            up = up_ref[start : start + tile, h * HD : (h + 1) * HD]
            low = probs_ref[0, h, start : start + tile, :]
            shared = jnp.sum(
                up.astype(F32) * scaled_ref[0, start : start + tile, h * HD : (h + 1) * HD], axis=1, keepdims=True
            )
            grads = (low.astype(F32) * (dot_nt(up, values) - shared)).astype(BF16)
            acts_ref[0, start : start + tile, ffn + h * HD : ffn + (h + 1) * HD] = (
                dot_nn(grads, keys) * (HD**-0.5)
            ).astype(BF16)
            key_sum = key_sum + dot_tn(query, grads)
            value_sum = value_sum + dot_tn(up, low)
        lane = ffn + width + h * HD
        acts_ref[0, :, lane : lane + HD] = key_sum.T.astype(BF16)
        lane = lane + width
        acts_ref[0, :, lane : lane + HD] = value_sum.T.astype(BF16)

    part_ref[...] = dot_nt(acts_ref[0], wcat_ref[...])

    channels(chan_ref, tok_ref.at[0], g, count, width, pad)

    @pl.when(step == 0)
    def _():
        tapsum_ref[...] = jnp.zeros(tapsum_ref.shape, F32)

    for start in range(0, length, 128):
        here = start + lax.broadcasted_iota(jnp.int32, (128, 1), 0)
        docs = doc_of(starts_ref, step, here)
        own = [ref[pad + start : pad + start + 128, :] for ref in conv_refs]
        back = jnp.zeros((128, width), F32)
        for shift in range(-3, 4):
            begin = pad + start + shift
            moved = chan_ref[begin : begin + 128, :]
            linked = docs == doc_of(starts_ref, step, here + shift)
            if shift != 0:
                moved = jnp.where(linked, moved, 0.0)
            base = 0
            mixed = jnp.zeros((128, width), F32)
            for k, taps in enumerate(TAPS):
                half = taps // 2
                if abs(shift) <= half:
                    tap = base + shift + half
                    tapsum_ref[tap : tap + 1, :] += jnp.sum(own[k] * moved, axis=0, keepdims=True)
                    tap = base - shift + half
                    mixed = mixed + conv_refs[k][begin : begin + 128, :] * taps_ref[tap : tap + 1, :]
                base += taps
            back = back + (jnp.where(linked, mixed, 0.0) if shift != 0 else mixed)
        for which in range(count):

            @pl.when(g == which)
            def _():
                part_ref[start : start + 128, which * width : (which + 1) * width] += back

    for k, out in enumerate((p0, p1, p2, p3)):
        out[0] = part_ref[pl.ds(pl.multiple_of((g ^ k) * rows, rows), rows), :].astype(BF16)


def block(shape):
    zeros = (0,) * (len(shape) - 1)
    return pl.BlockSpec((1,) + tuple(shape[1:]), lambda i: (i,) + zeros)


def whole(shape):
    zeros = (0,) * len(shape)
    return pl.BlockSpec(tuple(shape), lambda i: zeros)


def smem():
    return pl.BlockSpec(memory_space=pltpu.SMEM)


def struct(shape, dtype):
    return jax.ShapeDtypeStruct(tuple(shape), dtype)


def params():
    return pltpu.CompilerParams(dimension_semantics=("arbitrary",), vmem_limit_bytes=VMEM_LIMIT)


def local(
    groups, count, tokens, cotangent, path_masks, seg_starts, query_weight, key_weight, value_weight, output_weight,
    small_kernel, middle_kernel, large_kernel, small_mixer, middle_mixer, large_mixer, inner_weight, outer_weight,
    norm_gain, norm_bias,
):
    seqs, rows, dim = tokens.shape
    length = rows * count
    width = dim // count
    ffn = inner_weight.shape[1] // count
    wide = ffn + 4 * width
    heads = width // HD
    part = dim // groups
    batch, g = lax.axis_index("batch"), lax.axis_index("seq")
    g_arr = g.astype(jnp.int32).reshape(1)

    def send_seq(value, flip):
        return lax.ppermute(value, "seq", [(i, i ^ flip) for i in range(count)])

    def gather(value):
        far = send_seq(value, 2)
        near = send_seq(value, 1)
        return value, near, far, send_seq(far, 1)

    def columns(weight):
        return lax.dynamic_slice_in_dim(weight, g * (weight.shape[1] // count), weight.shape[1] // count, axis=1)

    def row_slice(weight):
        return lax.dynamic_slice_in_dim(weight, g * (weight.shape[0] // count), weight.shape[0] // count, axis=0)

    token_parts = gather(tokens)
    wqkv = jnp.concatenate([columns(query_weight), columns(key_weight), columns(value_weight)], axis=1)
    win = columns(inner_weight)
    wcat = jnp.concatenate([win, wqkv], axis=1)
    wrow = jnp.concatenate(
        [row_slice(w) for w in (outer_weight, output_weight, small_mixer, middle_mixer, large_mixer)], axis=0
    )
    taps = columns(
        jnp.concatenate([small_kernel, middle_kernel, large_kernel, jnp.zeros((1, dim), BF16)], axis=0)
    ).astype(F32)

    piece = (seqs, rows, dim)
    full = (seqs, length, dim)
    p0, p1, p2, p3, tok_full, mcat, slope, qkv, probs, scaled = pl.pallas_call(
        functools.partial(forward_kernel, count),
        grid=(seqs,),
        in_specs=[smem()] * 3
        + [block(piece)] * 4
        + [whole(wqkv.shape), whole(win.shape), whole(wrow.shape), whole(taps.shape)],
        out_specs=[block(piece)] * 4
        + [
            block(full),
            block((seqs, length, wide)),
            block((seqs, length, ffn)),
            block((seqs, length, 3 * width)),
            block((seqs, heads, length, length)),
            block((seqs, length, width)),
        ],
        out_shape=[struct(piece, BF16)] * 4
        + [
            struct(full, BF16),
            struct((seqs, length, wide), BF16),
            struct((seqs, length, ffn), F32),
            struct((seqs, length, 3 * width), BF16),
            struct((seqs, heads, length, length), BF16),
            struct((seqs, length, width), F32),
        ],
        scratch_shapes=[pltpu.VMEM((length + 16, width), F32), pltpu.VMEM((length, dim), F32)],
        compiler_params=params(),
    )(g_arr, path_masks, seg_starts, *token_parts, wqkv, win, wrow, taps)

    def scatter(a, b, c, d):
        away = send_seq(d, 1)
        near = send_seq(b, 1)
        far = send_seq((c.astype(F32) + away.astype(F32)).astype(BF16), 2)
        return a, near, far

    own, near, far = scatter(p0, p1, p2, p3)
    gain_row = norm_gain.reshape(1, dim)
    bias_row = norm_bias.reshape(1, dim)
    block_output, summed_grad, low_grad, norm_sums = pl.pallas_call(
        norm_kernel,
        grid=(seqs,),
        in_specs=[block(piece)] * 5 + [whole((1, dim))] * 2,
        out_specs=[block(piece)] * 3 + [whole((8, dim))],
        out_shape=[struct(piece, BF16), struct(piece, F32), struct(piece, BF16), struct((8, dim), F32)],
        compiler_params=params(),
    )(tokens, own, near, far, cotangent, gain_row, bias_row)

    low_parts = gather(low_grad)
    i0, i1, i2, i3, acts, tap_sums, low_full = pl.pallas_call(
        functools.partial(backward_kernel, count),
        grid=(seqs,),
        in_specs=[smem()] * 3
        + [block(piece)] * 4
        + [
            block(full),
            block((seqs, length, ffn)),
            block((seqs, length, 3 * width)),
            block((seqs, heads, length, length)),
            block((seqs, length, width)),
            whole(wrow.shape),
            whole(wcat.shape),
            whole(taps.shape),
        ],
        out_specs=[block(piece)] * 4 + [block((seqs, length, ffn + 3 * width)), whole(taps.shape), block(full)],
        out_shape=[struct(piece, BF16)] * 4
        + [struct((seqs, length, ffn + 3 * width), BF16), struct(taps.shape, F32), struct(full, BF16)],
        scratch_shapes=[pltpu.VMEM((length, width), BF16)]
        + [pltpu.VMEM((length + 16, width), F32)] * 4
        + [pltpu.VMEM((length, dim), F32)],
        compiler_params=params(),
    )(g_arr, path_masks, seg_starts, *low_parts, tok_full, slope, qkv, probs, scaled, wrow, wcat, taps)

    own, near, far = scatter(i0, i1, i2, i3)
    input_grad = (summed_grad + (own.astype(F32) + near.astype(F32) + far.astype(F32))).astype(BF16)

    all_rows = seqs * length
    low_rows = low_full.reshape(all_rows, dim)
    mcat_rows = mcat.reshape(all_rows, wide)
    outer_sum = dot_tn(mcat_rows[:, 0:ffn], low_rows)
    branch_sum = dot_tn(mcat_rows[:, ffn:], low_rows)
    tok_rows = tok_full.reshape(all_rows, dim)
    act_rows = acts.reshape(all_rows, ffn + 3 * width)
    inner_sum = dot_tn(tok_rows, act_rows[:, 0:ffn])
    qkv_sum = dot_tn(tok_rows, act_rows[:, ffn:])
    tap_rows = tap_sums.shape[0] - 1
    tap_cols = lax.dynamic_update_slice_in_dim(
        jnp.zeros((dim, tap_rows), F32), tap_sums[0:tap_rows].T, g * width, axis=0
    )
    op_counts = jnp.sum(path_masks, axis=0).astype(F32) * (g == 0).astype(F32)
    extra = jnp.concatenate(
        [tap_cols, norm_sums[0:2].T, jnp.broadcast_to(op_counts[None, :], (dim, op_counts.shape[0]))], axis=1
    )
    qkv_sum = jnp.concatenate([qkv_sum, extra], axis=1)

    bits = groups.bit_length() - 1
    top = count.bit_length() - 1

    def halve(value, bit):
        pre, blocks, r, w = value.shape
        split = value.reshape(pre, blocks // 2, 2, r, w)
        mine = (batch >> bit) & 1
        sent = lax.dynamic_index_in_dim(split, 1 - mine, axis=2, keepdims=False).astype(BF16)
        kept = lax.dynamic_index_in_dim(split, mine, axis=2, keepdims=False).astype(F32)
        got = lax.ppermute(sent, "batch", [(i, i ^ (1 << bit)) for i in range(groups)])
        return kept + got.astype(F32)

    def reduce_columns(value):
        value = value.reshape(1, groups, part, value.shape[1])
        for bit in range(bits):
            value = halve(value, bit)
        low = value[0, 0].astype(BF16)
        return jnp.stack(gather(low))

    def pairs(want):
        found = []
        for b in range(groups):
            for s in range(count):
                to = want(b, s)
                if to is not None:
                    found.append((b * count + s, to[0] * count + to[1]))
        return found

    def lead(b):
        return b >> (bits - top)

    def reduce_rows(value, pre):
        blocks = groups // count
        value = value.reshape(pre, blocks, value.shape[0] // (pre * blocks), value.shape[1])
        for bit in range(bits - top):
            value = halve(value, bit)
        for bit in range(top):
            level = bits - top + bit

            def target(b, s, bit=bit, level=level):
                settled = (lead(b) ^ s) & ((1 << bit) - 1)
                if settled or not ((lead(b) ^ s) >> bit) & 1:
                    return None
                return b ^ (1 << level), s

            got = lax.ppermute(value.astype(BF16), ("batch", "seq"), pairs(target))
            value = value + got.astype(F32)
        low = jnp.where(lead(batch) == g, value, 0.0).astype(BF16)
        low = low + lax.ppermute(
            low, ("batch", "seq"), pairs(lambda b, s: (b, s ^ 2) if s == lead(b) else None)
        )
        low = low + lax.ppermute(
            low, ("batch", "seq"), pairs(lambda b, s: (b, s ^ 1) if (s ^ lead(b)) & 1 == 0 else None)
        )
        return low[:, 0]

    outer_low = reduce_rows(outer_sum, 1)
    branch_low = reduce_rows(branch_sum, 4)
    inner_low = reduce_columns(inner_sum)
    qkv_low = reduce_columns(qkv_sum)

    def ordered(stack):
        return [lax.dynamic_index_in_dim(stack, g ^ k, axis=0, keepdims=False).astype(F32) for k in range(count)]

    inner_parts = ordered(inner_low)
    qkv_parts = ordered(qkv_low)
    extras = sum(p[:, 3 * width :] for p in qkv_parts)
    counts = extras[0, tap_rows + 2 :]
    query_grad, key_grad, value_grad = [
        jnp.concatenate([p[:, i * width : (i + 1) * width] for p in qkv_parts], axis=1) / counts[0] for i in range(3)
    ]
    inner_grad = jnp.concatenate(inner_parts, axis=1) / counts[4]
    outer_grad = outer_low[0].astype(F32) / counts[4]
    branch_f = branch_low.astype(F32)
    bounds = [0]
    for taps_k in TAPS:
        bounds.append(bounds[-1] + taps_k)
    kernel_grads = [(extras[:, bounds[k] : bounds[k + 1]] / counts[k + 1]).T for k in range(3)]
    return (
        block_output,
        input_grad,
        query_grad,
        key_grad,
        value_grad,
        branch_f[0] / counts[0],
        kernel_grads[0],
        kernel_grads[1],
        kernel_grads[2],
        branch_f[1] / counts[1],
        branch_f[2] / counts[2],
        branch_f[3] / counts[3],
        inner_grad,
        outer_grad,
        extras[:, tap_rows],
        extras[:, tap_rows + 1],
    )


def solution(mesh):
    rows = P("batch", "seq", None)
    groups = P("batch", None)
    in_specs = (rows, rows, groups, groups) + (P(),) * 14
    out_specs = (
        (rows, rows)
        + (groups,) * 4
        + (P(None, "batch"),) * 3
        + (groups,) * 5
        + (P("batch"), P("batch"))
    )
    body = functools.partial(local, mesh.shape["batch"], mesh.shape["seq"])
    return jax.shard_map(body, mesh=mesh, in_specs=in_specs, out_specs=out_specs, check_vma=False)
```

time: 1370 us -> 311 us (0.23)
  waiting for transfers between devices: 1030 us -> 85.1 us
  matrix products: 121 us -> 14.7 us
  Pallas kernels: 0 us -> 88.8 us
  local copies, waits for them, and re-layouts: 89.3 us -> 44.3 us
  blocking collectives: 42.1 us -> 0 us
  starting transfers between devices: 18.5 us -> 45.8 us
  other arithmetic: 49.4 us -> 30.1 us
  between operations: 16.1 us -> 1.25 us
    unnamed x25 -> x0, waiting for transfers between devices: 505 us -> none
    reduce_scatter x6 -> x0, waiting for transfers between devices: 432 us -> none  [the longest x1 166 us: local(): lax.psum_scatter(outer_sum, 'batch', scatter_dimension=0, tiled=True)]
    dot_general x33 -> x4, matrix products: 121 us -> 14.7 us  [dot_tn(): lax.dot_general(left, right, (((0,), (0,)), ((), ())), preferred_element_...]
    pallas_call x0 -> x3, Pallas kernels: none -> 88.8 us  [the longest x1 46.4 us: local(): pl.pallas_call(functools.partial(forward_kernel, count), grid=(seqs,), in...]
    psum x1 -> x0, waiting for transfers between devices: 85.9 us -> none  [local(): lax.psum((shares[0], shares[1], shares[2], shares[3], shares[4], shares[5...]
    ppermute x8 -> x34, waiting for transfers between devices: 0.02 us -> 85.1 us  [the longest x18 32.6 us: send_seq(): return lax.ppermute(value, 'seq', [(i, i ^ flip) for i in range(count)])]
    unnamed x138 -> x67, local copies, waits for them, and re-layouts: 55.7 us -> 11.6 us
    ppermute x8 -> x34, starting transfers between devices: 17.5 us -> 45.8 us  [the longest x18 19.8 us: send_seq(): return lax.ppermute(value, 'seq', [(i, i ^ flip) for i in range(count)])]
  transfers between devices with their start and end apart: 25 -> 34, of which waited for: 15 -> 12; matrix products, arithmetic and copies ran while one was open for 14% -> 26% of each run, Pallas kernels for 0% -> 0%
where the time goes in v1:
time: 311 us; the launch traced here: 310 us
  Pallas kernels  88.8 us (29%)
  waiting for transfers between devices  85.1 us (27%)
  starting transfers between devices  45.8 us (15%)
  local copies, waits for them, and re-layouts  44.3 us (14%)
  other arithmetic  30.1 us (10%)
  matrix products  14.7 us (5%)
    pallas_call x1, Pallas kernels, local(): pl.pallas_call(functools.partial(forward_kernel, count), grid=(seqs,), in...  46.4 us
    pallas_call x1, Pallas kernels, local(): pl.pallas_call(functools.partial(backward_kernel, count), grid=(seqs,), i...  37.6 us
    ppermute x18, waiting for transfers between devices, send_seq(): return lax.ppermute(value, 'seq', [(i, i ^ flip) for i in range(count)])  32.6 us
    ppermute x8, waiting for transfers between devices, halve(): lax.ppermute(sent, 'batch', [(i, i ^ 1 << bit) for i in range(groups)])  29 us
    ppermute x4, waiting for transfers between devices, reduce_rows(): got = lax.ppermute(value.astype(BF16), ('batch', 'seq'), pairs(target))  23.5 us
    ppermute x18, starting transfers between devices, send_seq(): return lax.ppermute(value, 'seq', [(i, i ^ flip) for i in range(count)])  19.8 us
    dot_general x4, local copies, waits for them, and re-layouts, dot_tn(): lax.dot_general(left, right, (((0,), (0,)), ((), ())), preferred_element_...  16 us
    dot_general x4, matrix products, dot_tn(): lax.dot_general(left, right, (((0,), (0,)), ((), ())), preferred_element_...  14.7 us
  transfers between devices with their start and end apart: 34, of which 12 were waited for; matrix products, arithmetic and copies ran while one was open for 26% of the time, Pallas kernels for 0%

profile of v1, /device:TPU:0, one launch (start us, length us, event | category | flops | bytes accessed | tf_op | source)
XLA Modules:
  0.0 310.1 jit_solution(18162580789991942010)
XLA Ops:
  0.7 3.0 collective-permute-start.1
  3.7 1.3 dynamic-slice_dynamic-update-slice_fusion
  8.3 1.6 constant_dynamic-slice_fusion.1
  9.8 7.4 %collective-permute-done.1.t2 = bf16[3,128,768]{2,1,0:T(8,128)(2,1)S(1)} collective-permute-done((bf16[3,128,768]{2,1,0:T(8,128)(2,1)}, bf16[3,128,768]{2,1,0:T(8,128)(2,1)S(1)}, u32[]{:S(2)}, u32[]{:S(2)}) %collective-permute-start.1) | collective-permute-done | bytes 589856 | tf_op jit(solution)/shard_map/ppermute | solution.py:298
  18.4 1.6 pad_maximum_fusion.wqkv_ref
  20.0 2.4 constant_dynamic-slice_fusion.win_ref
  24.1 46.4 %shard_map.297 = (bf16[3,128,768]{2,1,0:T(8,128)(2,1)}, bf16[3,128,768]{2,1,0:T(8,128)(2,1)}, bf16[3,128,768]{2,1,0:T(8,128)(2,1)}, bf16[3,128,768]{2,1,0:T(8,12...) custom-call(s32[1]{0:T(128)} %bitcast.g_ref, ...), custom_call_target="tpu_custom_call" | custom-call | tf_op jit(solution)/shard_map/pallas_call | solution.py:324
  71.2 1.8 collective-permute-done.4
  74.2 1.8 collective-permute-start.5
  77.2 12.7 %collective-permute-done.5.c_ref = bf16[3,128,768]{2,1,0:T(8,128)(2,1)S(1)} collective-permute-done((bf16[3,128,768]{2,1,0:T(8,128)(2,1)S(1)}, bf16[3,128,768]{2,1,0:T(8,128)(2,1)S(1)}, u32[]{:S(2)}, u32[]{:S(2)}) %collective-permute-start.5) | collective-permute-done | bytes 589856 | tf_op jit(solution)/shard_map/ppermute | solution.py:298
  90.7 4.8 %shard_map.298 = (bf16[3,128,768]{2,1,0:T(8,128)(2,1)}, f32[3,128,768]{2,1,0:T(8,128)}, bf16[3,128,768]{2,1,0:T(8,128)(2,1)}, f32[8,768]{1,0:T(8,128)}) custom-call(bf16[3,128,768]{2,1,0:T(8,128)(2,1)} %tok_ref.1, bf16[3,128,768]{2,1,0:T(8,128)(2,1)} %get-tuple-element.37.a_ref, bf16[3,128,768]{2,1,0:T(8,128)(2,1)} %copy-done.19, ...), custom_call_target="tpu_custom_call" | custom-call | tf_op jit(solution)/shard_map/pallas_call | solution.py:361
  95.5 1.8 collective-permute-start.7
  97.3 2.9 concatenate.34.wcat_ref
  100.5 10.3 %collective-permute-done.7.l2 = bf16[3,128,768]{2,1,0:T(8,128)(2,1)} collective-permute-done((bf16[3,128,768]{2,1,0:T(8,128)(2,1)}, bf16[3,128,768]{2,1,0:T(8,128)(2,1)}, u32[]{:S(2)}, u32[]{:S(2)}) %collective-permute-start.7) | collective-permute-done | bytes 589856 | tf_op jit(solution)/shard_map/ppermute | solution.py:298
  110.7 4.8 %slice_bitcast_fusion = (bf16[768,1536]{0,1:T(8,128)(2,1)}, bf16[768,1536]{0,1:T(8,128)(2,1)}) fusion(bf16[1536,1536]{1,0:T(8,128)(2,1)} %bitcast.120), kind=kLoop, calls=%fused_computation | loop fusion | bytes 9437184 | tf_op jit(solution)/shard_map/dot_general | solution.py:28
  115.5 4.4 %copy.50 = bf16[768,1536]{1,0:T(8,128)(2,1)} copy(bf16[768,1536]{0,1:T(8,128)(2,1)} %get-tuple-element.108) | data formatting | bytes 4718592 | tf_op jit(solution)/shard_map/dot_general | solution.py:28
  120.0 2.5 copy.49
  122.5 4.3 %copy.48 = bf16[768,1536]{1,0:T(8,128)(2,1)} copy(bf16[768,1536]{0,1:T(8,128)(2,1)} %get-tuple-element.109) | data formatting | bytes 4718592 | tf_op jit(solution)/shard_map/dot_general | solution.py:28
  128.5 37.6 %shard_map.299 = (bf16[3,128,768]{2,1,0:T(8,128)(2,1)}, bf16[3,128,768]{2,1,0:T(8,128)(2,1)}, bf16[3,128,768]{2,1,0:T(8,128)(2,1)}, bf16[3,128,768]{2,1,0:T(8,12...) custom-call(s32[1]{0:T(128)} %bitcast.g_ref, s32[3,5]{1,0:T(4,128)} %masks_ref.3, ...), custom_call_target="tpu_custom_call" | custom-call | tf_op jit(solution)/shard_map/pallas_call | solution.py:371
  166.2 3.8 %fusion.29 = f32[2,384,768]{2,1,0:T(8,128)S(1)} fusion(bf16[2,384,1536]{2,1,0:T(8,128)(2,1)S(1)} %bitcast.127, bf16[1536,768,1]{1,0,2:T(8,128)(2,1)} %bitcast.138), kind=kOutput, calls=%fused_computation.100 | convolution fusion | flops 1811939328 | bytes 7077888 | tf_op jit(solution)/shard_map/dot_general | solution.py:28
  170.9 1.7 collective-permute-start.29
  172.7 4.4 %fusion.1 = f32[768,576]{0,1:T(8,128)} fusion(bf16[1536,768]{1,0:T(8,128)(2,1)S(1)} %bitcast.117, bf16[1536,1344]{1,0:T(8,128)(2,1)} %bitcast.136), kind=kOutput, calls=%fused_computation.4 | convolution fusion | flops 1358954496 | bytes 6094848 | tf_op jit(solution)/shard_map/dot_general | solution.py:28
  177.5 1.7 maximum_maximum_fusion
  179.2 1.8 copy.47
  181.0 1.3 fusion.7
  182.6 4.5 %fusion = f32[4,2,96,768]{3,2,1,0:T(8,128)S(1)} fusion(bf16[4,2,96,1536]{3,2,1,0:T(8,128)(2,1)} %bitcast.126, bf16[1536,1344]{1,0:T(8,128)(2,1)} %bitcast.137), kind=kOutput, calls=%fused_computation.2 | convolution fusion | flops 1811939328 | bytes 7077888 | tf_op jit(solution)/shard_map/dot_general | solution.py:28
  187.2 1.8 collective-permute-start.23
  189.0 2.0 fusion.28
  192.3 4.7 %collective-permute-done.12 = bf16[1,4,96,598]{3,2,1,0:T(8,128)(2,1)S(1)} collective-permute-done((bf16[1,4,96,598]{3,2,1,0:T(8,128)(2,1)S(1)}, bf16[1,4,96,598]{3,2,1,0:T(8,128)(2,1)S(1)}, u32[]{:S(2)}, u32[]{:S(2)}) %collective-permute-start.12) | collective-permute-done | bytes 459296 | tf_op jit(solution)/shard_map/ppermute | solution.py:426
  197.0 1.9 collective-permute-start.9
  199.0 1.9 collective-permute-start.13
  201.1 8.6 %collective-permute-done.23 = bf16[1,4,96,768]{3,2,1,0:T(8,128)(2,1)S(1)} collective-permute-done((bf16[1,4,96,768]{3,2,1,0:T(8,128)(2,1)S(1)}, bf16[1,4,96,768]{3,2,1,0:T(8,128)(2,1)S(1)}, u32[]{:S(2)}, u32[]{:S(2)}) %collective-permute-start.23) | collective-permute-done | bytes 589856 | tf_op jit(solution)/shard_map/ppermute | solution.py:426
  209.7 1.3 collective-permute-start.30
  211.1 2.7 collective-permute-start.24
  213.9 8.3 %collective-permute-done.18 = bf16[4,1,96,768]{3,2,1,0:T(8,128)(2,1)S(1)} collective-permute-done((bf16[4,1,96,768]{3,2,1,0:T(8,128)(2,1)S(1)}, bf16[4,1,96,768]{3,2,1,0:T(8,128)(2,1)S(1)}, u32[]{:S(2)}, u32[]{:S(2)}) %collective-permute-start.18) | collective-permute-done | bytes 589856 | tf_op jit(solution)/shard_map/ppermute | solution.py:426
  222.3 2.8 collective-permute-start.14
  225.2 5.3 %collective-permute-done.14 = bf16[1,1,96,598]{3,2,1,0:T(8,128)(2,1)S(1)} collective-permute-done((bf16[1,1,96,598]{3,2,1,0:T(8,128)(2,1)S(1)}, bf16[1,1,96,598]{3,2,1,0:T(8,128)(2,1)S(1)}, u32[]{:S(2)}, u32[]{:S(2)}) %collective-permute-start.14) | collective-permute-done | bytes 114848 | tf_op jit(solution)/shard_map/ppermute | solution.py:426
  230.6 1.3 collective-permute-start.19
  231.9 1.9 collective-permute-start.16
  233.9 1.4 collective-permute-start.25
  236.8 3.0 collective-permute-start.15
  239.9 2.1 collective-permute-done.25
  241.9 2.1 collective-permute-start.17
  244.8 1.5 collective-permute-start.11
  248.1 1.5 maximum_divide_fusion.2
  249.6 1.3 fusion.16
  251.0 1.5 maximum_divide_fusion.1
  253.9 1.3 collective-permute-start.20
  255.4 1.3 collective-permute-start.31
  256.7 1.5 maximum_divide_fusion
  258.2 1.3 fusion.18
  259.4 19.8 %collective-permute-done.20 = bf16[4,1,96,768]{3,2,1,0:T(8,128)(2,1)S(1)} collective-permute-done((bf16[4,1,96,768]{3,2,1,0:T(8,128)(2,1)S(1)}, bf16[4,1,96,768]{3,2,1,0:T(8,128)(2,1)S(1)}, u32[]{:S(2)}, u32[]{:S(2)}) %collective-permute-start.20) | collective-permute-done | bytes 589856 | tf_op jit(solution)/shard_map/ppermute | solution.py:462
  279.5 2.2 collective-permute-start.21
  281.8 3.7 %collective-permute-done.31 = bf16[1,1,384,768]{3,2,1,0:T(8,128)(2,1)S(1)} collective-permute-done((bf16[1,1,384,768]{3,2,1,0:T(8,128)(2,1)S(1)}, bf16[1,1,384,768]{3,2,1,0:T(8,128)(2,1)S(1)}, u32[]{:S(2)}, u32[]{:S(2)}) %collective-permute-start.31) | collective-permute-done | bytes 589856 | tf_op jit(solution)/shard_map/ppermute | solution.py:462
  285.8 2.1 collective-permute-start.32
  288.7 1.5 copy.53
  290.1 1.5 copy.52
  291.6 1.4 copy.51
  293.6 2.3 add_convert_fusion
  297.1 2.0 collective-permute-start.22
  301.5 1.3 collective-permute-start.33
  302.8 1.8 convert_divide_fusion
  304.7 3.5 %fusion.11 = (f32[96,768]{1,0:T(8,128)}, f32[96,768]{1,0:T(8,128)}, f32[96,768]{1,0:T(8,128)}, f32[96,768]{1,0:T(8,128)}) fusion(f32[4,1,96,768]{3,2,1,0:T(8,128)S(1)} %add_convert_fusion.3, f32[]{:T(128)} %bitcast.36, f32[]{:T(128)} %bitcast.34, f32[]{:T(128)} %bitcast.32, f32[]{:T(128)} %bitcast.24), kind=kLoop, calls=%fused_computation.42 | loop fusion | flops 294912 | bytes 2359312 | tf_op jit(solution)/shard_map/div | solution.py:507
  308.2 1.8 divide_bitcast_fusion
  (147 shorter events, 27.0 us)
Async XLA Ops:
  0.6 7.4 %copy-start = (bf16[768,768]{1,0:T(8,128)(2,1)S(1)}, bf16[768,768]{1,0:T(8,128)(2,1)}, u32[]{:S(2)}) copy-start(bf16[768,768]{1,0:T(8,128)(2,1)} %param.22) | copy-start | bytes 3538948
  0.7 16.5 %collective-permute-start.1 = (bf16[3,128,768]{2,1,0:T(8,128)(2,1)}, bf16[3,128,768]{2,1,0:T(8,128)(2,1)S(1)}, u32[]{:S(2)}, u32[]{:S(2)}) collective-permute-start(bf16[3,128,768]{2,1,0:T(8,128)(2,1)} %tok_ref.1), channel_id=1, source_target_pairs={{0,2},{1,3},{2,0},{3,1},{4,6},{5,7},{6,4},{7,5},{8,10},{9,11},{10,... | collective-permute-start | bytes 1769480 | tf_op jit(solution)/shard_map/ppermute | solution.py:298
  3.7 19.4 %collective-permute-start = (bf16[3,128,768]{2,1,0:T(8,128)(2,1)}, bf16[3,128,768]{2,1,0:T(8,128)(2,1)S(1)}, u32[]{:S(2)}, u32[]{:S(2)}) collective-permute-start(bf16[3,128,768]{2,1,0:T(8,128)(2,1)} %tok_ref.1), channel_id=1, source_target_pairs={{0,1},{1,0},{2,3},{3,2},{4,5},{5,4},{6,7},{7,6},{8,9},{9,8},{10,11... | collective-permute-start | bytes 1769480 | tf_op jit(solution)/shard_map/ppermute | solution.py:298
  17.2 5.2 %copy-start.12 = (bf16[3,128,768]{2,1,0:T(8,128)(2,1)}, bf16[3,128,768]{2,1,0:T(8,128)(2,1)S(1)}, u32[]{:S(2)}) copy-start(bf16[3,128,768]{2,1,0:T(8,128)(2,1)S(1)} %collective-permute-done.1.t2) | copy-start | bytes 1769476
  17.2 5.9 %collective-permute-start.2 = (bf16[3,128,768]{2,1,0:T(8,128)(2,1)S(1)}, bf16[3,128,768]{2,1,0:T(8,128)(2,1)S(1)}, u32[]{:S(2)}, u32[]{:S(2)}) collective-permute-start(bf16[3,128,768]{2,1,0:T(8,128)(2,1)S(1)} %collective-permute-done.1.t2), channel_id=1, source_target_pairs={{0,1},{1,0},{2,3},{3,2},{4,5},{5,4},{6,7},{7,6},{8,9},{9,8},{10,11... | collective-permute-start | bytes 1769480 | tf_op jit(solution)/shard_map/ppermute | solution.py:298
  18.4 4.0 %copy-start.2 = (bf16[1536,768]{1,0:T(8,128)(2,1)}, bf16[1536,768]{1,0:T(8,128)(2,1)S(1)}, u32[]{:S(2)}) copy-start(bf16[1536,768]{1,0:T(8,128)(2,1)S(1)} %dynamic-slice_dynamic-update-slice_fusion.1.wrow_ref) | copy-start | bytes 7077892
  18.4 4.0 %copy-start.23 = (bf16[5,768]{1,0:T(8,128)(2,1)S(1)}, bf16[5,768]{1,0:T(8,128)(2,1)}, u32[]{:S(2)}) copy-start(bf16[5,768]{1,0:T(8,128)(2,1)} %param.27) | copy-start | bytes 23044
  18.4 4.0 %copy-start.24 = (bf16[7,768]{1,0:T(8,128)(2,1)S(1)}, bf16[7,768]{1,0:T(8,128)(2,1)}, u32[]{:S(2)}) copy-start(bf16[7,768]{1,0:T(8,128)(2,1)} %param.28) | copy-start | bytes 32260
  18.4 4.0 %copy-start.25 = (bf16[3,768]{1,0:T(4,128)(2,1)S(1)}, bf16[3,768]{1,0:T(4,128)(2,1)}, u32[]{:S(2)}) copy-start(bf16[3,768]{1,0:T(4,128)(2,1)} %param.26) | copy-start | bytes 13828
  23.1 0.8 copy-start.13
  23.1 1.0 copy-start.16
  24.1 51.9 %copy-start.26 = (bf16[768]{0:T(1024)(128)(2,1)S(1)}, bf16[768]{0:T(1024)(128)(2,1)}, u32[]{:S(2)}) copy-start(bf16[768]{0:T(1024)(128)(2,1)} %param.34) | copy-start | bytes 4612
  24.1 52.5 %copy-start.27 = (bf16[768]{0:T(1024)(128)(2,1)S(1)}, bf16[768]{0:T(1024)(128)(2,1)}, u32[]{:S(2)}) copy-start(bf16[768]{0:T(1024)(128)(2,1)} %param.35) | copy-start | bytes 4612
  70.5 2.5 collective-permute-start.4
  71.1 6.1 %collective-permute-start.3 = (bf16[3,128,768]{2,1,0:T(8,128)(2,1)}, bf16[3,128,768]{2,1,0:T(8,128)(2,1)S(1)}, u32[]{:S(2)}, u32[]{:S(2)}) collective-permute-start(bf16[3,128,768]{2,1,0:T(8,128)(2,1)} %get-tuple-element.38), channel_id=1, source_target_pairs={{0,1},{1,0},{2,3},{3,2},{4,5},{5,4},{6,7},{7,6},{8,9},{9,8},{10,11... | collective-permute-start | bytes 1769480 | tf_op jit(solution)/shard_map/ppermute | solution.py:298
  74.2 23.2 %copy-start.3 = (bf16[768,768]{1,0:T(8,128)(2,1)S(1)}, bf16[768,768]{1,0:T(8,128)(2,1)}, u32[]{:S(2)}) copy-start(bf16[768,768]{1,0:T(8,128)(2,1)} %constant_dynamic-slice_fusion.win_ref) | copy-start | bytes 3538948
  74.2 15.7 %collective-permute-start.5 = (bf16[3,128,768]{2,1,0:T(8,128)(2,1)S(1)}, bf16[3,128,768]{2,1,0:T(8,128)(2,1)S(1)}, u32[]{:S(2)}, u32[]{:S(2)}) collective-permute-start(bf16[3,128,768]{2,1,0:T(8,128)(2,1)S(1)} %add_convert_fusion.2), channel_id=1, source_target_pairs={{0,2},{1,3},{2,0},{3,1},{4,6},{5,7},{6,4},{7,5},{8,10},{9,11},{10,... | collective-permute-start | bytes 1769480 | tf_op jit(solution)/shard_map/ppermute | solution.py:298
  77.2 12.7 %copy-start.19 = (bf16[3,128,768]{2,1,0:T(8,128)(2,1)}, bf16[3,128,768]{2,1,0:T(8,128)(2,1)S(1)}, u32[]{:S(2)}) copy-start(bf16[3,128,768]{2,1,0:T(8,128)(2,1)S(1)} %collective-permute-done.3.b_ref) | copy-start | bytes 1769476
  89.9 0.8 copy-start.20
  95.5 4.8 %copy-start.21 = (s32[3,5]{1,0:T(4,128)S(1)}, s32[3,5]{1,0:T(4,128)}, u32[]{:S(2)}) copy-start(s32[3,5]{1,0:T(4,128)} %masks_ref.3) | copy-start | bytes 184
  95.5 15.2 %collective-permute-start.7 = (bf16[3,128,768]{2,1,0:T(8,128)(2,1)}, bf16[3,128,768]{2,1,0:T(8,128)(2,1)}, u32[]{:S(2)}, u32[]{:S(2)}) collective-permute-start(bf16[3,128,768]{2,1,0:T(8,128)(2,1)} %get-tuple-element.43.l0), channel_id=1, source_target_pairs={{0,2},{1,3},{2,0},{3,1},{4,6},{5,7},{6,4},{7,5},{8,10},{9,11},{10,... | collective-permute-start | bytes 1769480 | tf_op jit(solution)/shard_map/ppermute | solution.py:298
  100.4 27.1 %collective-permute-start.6 = (bf16[3,128,768]{2,1,0:T(8,128)(2,1)}, bf16[3,128,768]{2,1,0:T(8,128)(2,1)S(1)}, u32[]{:S(2)}, u32[]{:S(2)}) collective-permute-start(bf16[3,128,768]{2,1,0:T(8,128)(2,1)} %get-tuple-element.43.l0), channel_id=1, source_target_pairs={{0,1},{1,0},{2,3},{3,2},{4,5},{5,4},{6,7},{7,6},{8,9},{9,8},{10,11... | collective-permute-start | bytes 1769480 | tf_op jit(solution)/shard_map/ppermute | solution.py:298
  110.7 16.8 %collective-permute-start.8 = (bf16[3,128,768]{2,1,0:T(8,128)(2,1)}, bf16[3,128,768]{2,1,0:T(8,128)(2,1)S(1)}, u32[]{:S(2)}, u32[]{:S(2)}) collective-permute-start(bf16[3,128,768]{2,1,0:T(8,128)(2,1)} %collective-permute-done.7.l2), channel_id=1, source_target_pairs={{0,1},{1,0},{2,3},{3,2},{4,5},{5,4},{6,7},{7,6},{8,9},{9,8},{10,11... | collective-permute-start | bytes 1769480 | tf_op jit(solution)/shard_map/ppermute | solution.py:298
  115.5 4.4 %copy-start.4 = (bf16[3,512,768]{2,1,0:T(8,128)(2,1)S(1)}, bf16[3,512,768]{2,1,0:T(8,128)(2,1)}, u32[]{:S(2)}) copy-start(bf16[3,512,768]{2,1,0:T(8,128)(2,1)} %get-tuple-element.44.tok_ref) | copy-start | bytes 7077892
  127.5 0.8 copy-start.14
  127.5 1.0 copy-start.15
  128.5 37.6 %copy-start.10 = (bf16[768,1536]{1,0:T(8,128)(2,1)S(1)}, bf16[768,1536]{1,0:T(8,128)(2,1)}, u32[]{:S(2)}) copy-start(bf16[768,1536]{1,0:T(8,128)(2,1)} %copy.50) | copy-start | bytes 7077892
  166.2 6.5 %copy-start.22 = (f32[16,192]{1,0:T(8,128)S(1)}, f32[16,192]{1,0:T(8,128)}, u32[]{:S(2)}) copy-start(f32[16,192]{1,0:T(8,128)} %get-tuple-element.54) | copy-start | bytes 36868
  166.2 6.5 %copy-start.5 = (bf16[3,512,768]{2,1,0:T(8,128)(2,1)S(1)}, bf16[3,512,768]{2,1,0:T(8,128)(2,1)}, u32[]{:S(2)}) copy-start(bf16[3,512,768]{2,1,0:T(8,128)(2,1)} %get-tuple-element.44.tok_ref) | copy-start | bytes 7077892
  170.0 7.2 %copy-start.6 = (f32[2,384,768]{2,1,0:T(8,128)}, f32[2,384,768]{2,1,0:T(8,128)S(1)}, u32[]{:S(2)}) copy-start(f32[2,384,768]{2,1,0:T(8,128)S(1)} %fusion.29) | copy-start | bytes 7077892
  170.9 28.1 %collective-permute-start.29 = (bf16[1,1,384,768]{3,2,1,0:T(8,128)(2,1)}, bf16[1,1,384,768]{3,2,1,0:T(8,128)(2,1)S(1)}, u32[]{:S(2)}, u32[]{:S(2)}) collective-permute-start(bf16[1,1,384,768]{3,2,1,0:T(8,128)(2,1)} %fusion.6), channel_id=1, source_target_pairs={{0,4},{4,0},{8,12},{12,8},{16,20},{20,16},{24,28},{28,24},{1,5},{5... | collective-permute-start | bytes 1769480 | tf_op jit(solution)/shard_map/ppermute | solution.py:426
  182.2 14.8 %collective-permute-start.12 = (bf16[1,4,96,598]{3,2,1,0:T(8,128)(2,1)S(1)}, bf16[1,4,96,598]{3,2,1,0:T(8,128)(2,1)S(1)}, u32[]{:S(2)}, u32[]{:S(2)}) collective-permute-start(bf16[1,4,96,598]{3,2,1,0:T(8,128)(2,1)S(1)} %fusion.7), channel_id=1, source_target_pairs={{0,4},{4,0},{8,12},{12,8},{16,20},{20,16},{24,28},{28,24},{1,5},{5... | collective-permute-start | bytes 1377800 | tf_op jit(solution)/shard_map/ppermute | solution.py:426
  182.6 6.4 %copy-start.9 = (bf16[768,1536]{1,0:T(8,128)(2,1)S(1)}, bf16[768,1536]{1,0:T(8,128)(2,1)}, u32[]{:S(2)}) copy-start(bf16[768,1536]{1,0:T(8,128)(2,1)} %copy.48) | copy-start | bytes 7077892
  182.6 6.4 %copy-start.28 = (bf16[3,512,768]{2,1,0:T(8,128)(2,1)S(1)}, bf16[3,512,768]{2,1,0:T(8,128)(2,1)}, u32[]{:S(2)}) copy-start(bf16[3,512,768]{2,1,0:T(8,128)(2,1)} %get-tuple-element.57) | copy-start | bytes 7077892
  187.2 22.5 %collective-permute-start.23 = (bf16[1,4,96,768]{3,2,1,0:T(8,128)(2,1)S(1)}, bf16[1,4,96,768]{3,2,1,0:T(8,128)(2,1)S(1)}, u32[]{:S(2)}, u32[]{:S(2)}) collective-permute-start(bf16[1,4,96,768]{3,2,1,0:T(8,128)(2,1)S(1)} %fusion.5), channel_id=1, source_target_pairs={{0,4},{4,0},{8,12},{12,8},{16,20},{20,16},{24,28},{28,24},{1,5},{5... | collective-permute-start | bytes 1769480 | tf_op jit(solution)/shard_map/ppermute | solution.py:426
  189.0 2.4 copy-start.29
  189.0 9.9 %copy-start.8 = (f32[768,598]{1,0:T(8,128)S(1)}, f32[768,598]{1,0:T(8,128)}, u32[]{:S(2)}) copy-start(f32[768,598]{1,0:T(8,128)} %copy.47) | copy-start | bytes 5511172
  191.0 9.9 %copy-start.7 = (f32[2,384,768]{2,1,0:T(8,128)S(1)}, f32[2,384,768]{2,1,0:T(8,128)}, u32[]{:S(2)}) copy-start(f32[2,384,768]{2,1,0:T(8,128)} %copy-done.6) | copy-start | bytes 7077892
  191.1 31.2 %collective-permute-start.18 = (bf16[4,1,96,768]{3,2,1,0:T(8,128)(2,1)S(1)}, bf16[4,1,96,768]{3,2,1,0:T(8,128)(2,1)S(1)}, u32[]{:S(2)}, u32[]{:S(2)}) collective-permute-start(bf16[4,1,96,768]{3,2,1,0:T(8,128)(2,1)S(1)} %dynamic-slice_convert_fusion.2), channel_id=1, source_target_pairs={{0,4},{4,0},{8,12},{12,8},{16,20},{20,16},{24,28},{28,24},{1,5},{5... | collective-permute-start | bytes 1769480 | tf_op jit(solution)/shard_map/ppermute | solution.py:426
  191.4 42.5 %collective-permute-start.10 = (bf16[3,128,768]{2,1,0:T(8,128)(2,1)S(1)}, bf16[3,128,768]{2,1,0:T(8,128)(2,1)S(1)}, u32[]{:S(2)}, u32[]{:S(2)}) collective-permute-start(bf16[3,128,768]{2,1,0:T(8,128)(2,1)S(1)} %copy-done.29), channel_id=1, source_target_pairs={{0,1},{1,0},{2,3},{3,2},{4,5},{5,4},{6,7},{7,6},{8,9},{9,8},{10,11... | collective-permute-start | bytes 1769480 | tf_op jit(solution)/shard_map/ppermute | solution.py:298
  197.0 96.0 %collective-permute-start.9 = (bf16[3,128,768]{2,1,0:T(8,128)(2,1)}, bf16[3,128,768]{2,1,0:T(8,128)(2,1)}, u32[]{:S(2)}, u32[]{:S(2)}) collective-permute-start(bf16[3,128,768]{2,1,0:T(8,128)(2,1)} %get-tuple-element.50), channel_id=1, source_target_pairs={{0,1},{1,0},{2,3},{3,2},{4,5},{5,4},{6,7},{7,6},{8,9},{9,8},{10,11... | collective-permute-start | bytes 1769480 | tf_op jit(solution)/shard_map/ppermute | solution.py:298
  199.0 12.1 %collective-permute-start.13 = (bf16[1,2,96,598]{3,2,1,0:T(8,128)(2,1)S(1)}, bf16[1,2,96,598]{3,2,1,0:T(8,128)(2,1)S(1)}, u32[]{:S(2)}, u32[]{:S(2)}) collective-permute-start(bf16[1,2,96,598]{3,2,1,0:T(8,128)(2,1)S(1)} %fusion.15), channel_id=1, source_target_pairs={{0,8},{4,12},{8,0},{12,4},{16,24},{20,28},{24,16},{28,20},{1,9},{5... | collective-permute-start | bytes 688904 | tf_op jit(solution)/shard_map/ppermute | solution.py:426
  209.7 45.5 %collective-permute-start.30 = (bf16[1,1,384,768]{3,2,1,0:T(8,128)(2,1)S(1)}, bf16[1,1,384,768]{3,2,1,0:T(8,128)(2,1)S(1)}, u32[]{:S(2)}, u32[]{:S(2)}) collective-permute-start(bf16[1,1,384,768]{3,2,1,0:T(8,128)(2,1)S(1)} %fusion.9), channel_id=1, source_target_pairs={{1,9},{3,11},{5,13},{7,15},{8,0},{10,2},{12,4},{14,6},{17,25},{19,... | collective-permute-start | bytes 1769480 | tf_op jit(solution)/shard_map/ppermute | solution.py:462
  211.1 20.8 %collective-permute-start.24 = (bf16[1,2,96,768]{3,2,1,0:T(8,128)(2,1)S(1)}, bf16[1,2,96,768]{3,2,1,0:T(8,128)(2,1)S(1)}, u32[]{:S(2)}, u32[]{:S(2)}) collective-permute-start(bf16[1,2,96,768]{3,2,1,0:T(8,128)(2,1)S(1)} %fusion.10), channel_id=1, source_target_pairs={{0,8},{4,12},{8,0},{12,4},{16,24},{20,28},{24,16},{28,20},{1,9},{5... | collective-permute-start | bytes 884744 | tf_op jit(solution)/shard_map/ppermute | solution.py:426
  213.9 21.4 %copy-start.18 = (bf16[3,128,768]{2,1,0:T(8,128)(2,1)S(1)}, bf16[3,128,768]{2,1,0:T(8,128)(2,1)}, u32[]{:S(2)}) copy-start(bf16[3,128,768]{2,1,0:T(8,128)(2,1)} %get-tuple-element.51) | copy-start | bytes 1769476
  222.3 8.3 %collective-permute-start.14 = (bf16[1,1,96,598]{3,2,1,0:T(8,128)(2,1)S(1)}, bf16[1,1,96,598]{3,2,1,0:T(8,128)(2,1)S(1)}, u32[]{:S(2)}, u32[]{:S(2)}) collective-permute-start(bf16[1,1,96,598]{3,2,1,0:T(8,128)(2,1)S(1)} %dynamic-slice_convert_fusion.7), channel_id=1, source_target_pairs={{0,16},{4,20},{8,24},{12,28},{16,0},{20,4},{24,8},{28,12},{1,17},{... | collective-permute-start | bytes 344456 | tf_op jit(solution)/shard_map/ppermute | solution.py:426
  230.6 23.1 %collective-permute-start.19 = (bf16[4,1,96,768]{3,2,1,0:T(8,128)(2,1)S(1)}, bf16[4,1,96,768]{3,2,1,0:T(8,128)(2,1)S(1)}, u32[]{:S(2)}, u32[]{:S(2)}) collective-permute-start(bf16[4,1,96,768]{3,2,1,0:T(8,128)(2,1)S(1)} %fusion.8), channel_id=1, source_target_pairs={{1,9},{3,11},{5,13},{7,15},{8,0},{10,2},{12,4},{14,6},{17,25},{19,... | collective-permute-start | bytes 1769480 | tf_op jit(solution)/shard_map/ppermute | solution.py:462
  231.9 4.9 %collective-permute-start.16 = (bf16[96,598]{1,0:T(8,128)(2,1)S(1)}, bf16[96,598]{1,0:T(8,128)(2,1)S(1)}, u32[]{:S(2)}, u32[]{:S(2)}) collective-permute-start(bf16[96,598]{1,0:T(8,128)(2,1)S(1)} %bitcast.128), channel_id=1, source_target_pairs={{0,2},{1,3},{2,0},{3,1},{4,6},{5,7},{6,4},{7,5},{8,10},{9,11},{10,... | collective-permute-start | bytes 344456 | tf_op jit(solution)/shard_map/ppermute | solution.py:298
  233.9 8.0 %collective-permute-start.25 = (bf16[1,1,96,768]{3,2,1,0:T(8,128)(2,1)S(1)}, bf16[1,1,96,768]{3,2,1,0:T(8,128)(2,1)S(1)}, u32[]{:S(2)}, u32[]{:S(2)}) collective-permute-start(bf16[1,1,96,768]{3,2,1,0:T(8,128)(2,1)S(1)} %dynamic-slice_convert_fusion.6), channel_id=1, source_target_pairs={{0,16},{4,20},{8,24},{12,28},{16,0},{20,4},{24,8},{28,12},{1,17},{... | collective-permute-start | bytes 442376 | tf_op jit(solution)/shard_map/ppermute | solution.py:426
  236.8 7.9 %collective-permute-start.15 = (bf16[96,598]{1,0:T(8,128)(2,1)S(1)}, bf16[96,598]{1,0:T(8,128)(2,1)S(1)}, u32[]{:S(2)}, u32[]{:S(2)}) collective-permute-start(bf16[96,598]{1,0:T(8,128)(2,1)S(1)} %bitcast.129), channel_id=1, source_target_pairs={{0,1},{1,0},{2,3},{3,2},{4,5},{5,4},{6,7},{7,6},{8,9},{9,8},{10,11... | collective-permute-start | bytes 344456 | tf_op jit(solution)/shard_map/ppermute | solution.py:298
  241.9 4.3 %collective-permute-start.17 = (bf16[96,598]{1,0:T(8,128)(2,1)S(1)}, bf16[96,598]{1,0:T(8,128)(2,1)S(1)}, u32[]{:S(2)}, u32[]{:S(2)}) collective-permute-start(bf16[96,598]{1,0:T(8,128)(2,1)S(1)} %collective-permute-done.16), channel_id=1, source_target_pairs={{0,1},{1,0},{2,3},{3,2},{4,5},{5,4},{6,7},{7,6},{8,9},{9,8},{10,11... | collective-permute-start | bytes 344456 | tf_op jit(solution)/shard_map/ppermute | solution.py:298
  244.8 48.8 %collective-permute-start.11 = (bf16[3,128,768]{2,1,0:T(8,128)(2,1)}, bf16[3,128,768]{2,1,0:T(8,128)(2,1)}, u32[]{:S(2)}, u32[]{:S(2)}) collective-permute-start(bf16[3,128,768]{2,1,0:T(8,128)(2,1)} %add_convert_fusion.1), channel_id=1, source_target_pairs={{0,2},{1,3},{2,0},{3,1},{4,6},{5,7},{6,4},{7,5},{8,10},{9,11},{10,... | collective-permute-start | bytes 1769480 | tf_op jit(solution)/shard_map/ppermute | solution.py:298
  246.3 46.8 %collective-permute-start.27 = (bf16[96,768]{1,0:T(8,128)(2,1)}, bf16[96,768]{1,0:T(8,128)(2,1)}, u32[]{:S(2)}, u32[]{:S(2)}) collective-permute-start(bf16[96,768]{1,0:T(8,128)(2,1)} %bitcast.51), channel_id=1, source_target_pairs={{0,2},{1,3},{2,0},{3,1},{4,6},{5,7},{6,4},{7,5},{8,10},{9,11},{10,... | collective-permute-start | bytes 442376 | tf_op jit(solution)/shard_map/ppermute | solution.py:298
  253.9 25.3 %collective-permute-start.20 = (bf16[4,1,96,768]{3,2,1,0:T(8,128)(2,1)S(1)}, bf16[4,1,96,768]{3,2,1,0:T(8,128)(2,1)S(1)}, u32[]{:S(2)}, u32[]{:S(2)}) collective-permute-start(bf16[4,1,96,768]{3,2,1,0:T(8,128)(2,1)S(1)} %fusion.3), channel_id=1, source_target_pairs={{2,18},{6,22},{11,27},{15,31},{16,0},{20,4},{25,9},{29,13}} | collective-permute-start | bytes 1769480 | tf_op jit(solution)/shard_map/ppermute | solution.py:462
  255.4 30.1 %collective-permute-start.31 = (bf16[1,1,384,768]{3,2,1,0:T(8,128)(2,1)S(1)}, bf16[1,1,384,768]{3,2,1,0:T(8,128)(2,1)S(1)}, u32[]{:S(2)}, u32[]{:S(2)}) collective-permute-start(bf16[1,1,384,768]{3,2,1,0:T(8,128)(2,1)S(1)} %fusion.4), channel_id=1, source_target_pairs={{2,18},{6,22},{11,27},{15,31},{16,0},{20,4},{25,9},{29,13}} | collective-permute-start | bytes 1769480 | tf_op jit(solution)/shard_map/ppermute | solution.py:462
  279.5 14.1 %copy-start.11 = (f32[3,128,768]{2,1,0:T(8,128)S(1)}, f32[3,128,768]{2,1,0:T(8,128)}, u32[]{:S(2)}) copy-start(f32[3,128,768]{2,1,0:T(8,128)} %get-tuple-element.42) | copy-start | bytes 3538948
  279.5 14.1 %copy-start.17 = (bf16[3,128,768]{2,1,0:T(8,128)(2,1)S(1)}, bf16[3,128,768]{2,1,0:T(8,128)(2,1)}, u32[]{:S(2)}) copy-start(bf16[3,128,768]{2,1,0:T(8,128)(2,1)} %get-tuple-element.49) | copy-start | bytes 1769476
  279.5 16.4 %collective-permute-start.21 = (bf16[4,1,96,768]{3,2,1,0:T(8,128)(2,1)S(1)}, bf16[4,1,96,768]{3,2,1,0:T(8,128)(2,1)}, u32[]{:S(2)}, u32[]{:S(2)}) collective-permute-start(bf16[4,1,96,768]{3,2,1,0:T(8,128)(2,1)S(1)} %select_convert_fusion.1), channel_id=1, source_target_pairs={{0,2},{4,6},{9,11},{13,15},{18,16},{22,20},{27,25},{31,29}} | collective-permute-start | bytes 1769480 | tf_op jit(solution)/shard_map/ppermute | solution.py:465
  285.8 14.4 %collective-permute-start.32 = (bf16[1,1,384,768]{3,2,1,0:T(8,128)(2,1)S(1)}, bf16[1,1,384,768]{3,2,1,0:T(8,128)(2,1)}, u32[]{:S(2)}, u32[]{:S(2)}) collective-permute-start(bf16[1,1,384,768]{3,2,1,0:T(8,128)(2,1)S(1)} %select_convert_fusion), channel_id=1, source_target_pairs={{0,2},{4,6},{9,11},{13,15},{18,16},{22,20},{27,25},{31,29}} | collective-permute-start | bytes 1769480 | tf_op jit(solution)/shard_map/ppermute | solution.py:465
  293.1 6.1 %collective-permute-start.26 = (bf16[96,768]{1,0:T(8,128)(2,1)}, bf16[96,768]{1,0:T(8,128)(2,1)S(1)}, u32[]{:S(2)}, u32[]{:S(2)}) collective-permute-start(bf16[96,768]{1,0:T(8,128)(2,1)} %bitcast.51), channel_id=1, source_target_pairs={{0,1},{1,0},{2,3},{3,2},{4,5},{5,4},{6,7},{7,6},{8,9},{9,8},{10,11... | collective-permute-start | bytes 442376 | tf_op jit(solution)/shard_map/ppermute | solution.py:298
  293.1 6.1 %collective-permute-start.28 = (bf16[96,768]{1,0:T(8,128)(2,1)}, bf16[96,768]{1,0:T(8,128)(2,1)S(1)}, u32[]{:S(2)}, u32[]{:S(2)}) collective-permute-start(bf16[96,768]{1,0:T(8,128)(2,1)} %collective-permute-done.27), channel_id=1, source_target_pairs={{0,1},{1,0},{2,3},{3,2},{4,5},{5,4},{6,7},{7,6},{8,9},{9,8},{10,11... | collective-permute-start | bytes 442376 | tf_op jit(solution)/shard_map/ppermute | solution.py:298
  297.1 7.5 %collective-permute-start.22 = (bf16[4,1,96,768]{3,2,1,0:T(8,128)(2,1)S(1)}, bf16[4,1,96,768]{3,2,1,0:T(8,128)(2,1)S(1)}, u32[]{:S(2)}, u32[]{:S(2)}) collective-permute-start(bf16[4,1,96,768]{3,2,1,0:T(8,128)(2,1)S(1)} %add.170), channel_id=1, source_target_pairs={{0,1},{2,3},{4,5},{6,7},{9,8},{11,10},{13,12},{15,14},{16,17},{18,... | collective-permute-start | bytes 1769480 | tf_op jit(solution)/shard_map/ppermute | solution.py:468
  301.5 6.8 %collective-permute-start.33 = (bf16[1,1,384,768]{3,2,1,0:T(8,128)(2,1)S(1)}, bf16[1,1,384,768]{3,2,1,0:T(8,128)(2,1)S(1)}, u32[]{:S(2)}, u32[]{:S(2)}) collective-permute-start(bf16[1,1,384,768]{3,2,1,0:T(8,128)(2,1)S(1)} %add.178), channel_id=1, source_target_pairs={{0,1},{2,3},{4,5},{6,7},{9,8},{11,10},{13,12},{15,14},{16,17},{18,... | collective-permute-start | bytes 1769480 | tf_op jit(solution)/shard_map/ppermute | solution.py:468
  304.6 5.5 %copy-start.1 = (bf16[768,768]{1,0:T(8,128)(2,1)S(1)}, bf16[768,768]{1,0:T(8,128)(2,1)}, u32[]{:S(2)}) copy-start(bf16[768,768]{1,0:T(8,128)(2,1)} %param.22) | copy-start | bytes 3538948
